TPU v7x, 256 devices: a whole 4x4x8 slice. The times are simulated.
256 devices in a mesh: lat: 8 (over x_hi, y), lon: 32 (over z, x_lo, core).
Axes of the slice: x: 4 (x_hi: 2, x_lo: 2; x = x_hi * 2 + x_lo), y: 4, z: 8, core: 2. Of those that a mesh axis runs over, the one named last changes fastest.
Arguments:
- fields: bfloat16 [4, 192, 384, 192], P(None, 'lat', 'lon'), may hold values from -43 to 43, as said below
- out_grad: bfloat16 [4, 192, 384, 192], P(None, 'lat', 'lon'), may hold values from -6 to 6
- gain: float32 [192], replicated, may hold values from 0.5 to 1.5
- qkv_weight: bfloat16 [192, 576], replicated, may hold values from -0.4375 to 0.4375
- out_weight: bfloat16 [192, 192], replicated, may hold values from -0.4375 to 0.4375
- window_bias: float32 [16, 2, 6, 20736], P('lat'), may hold values from -4 to 454
Outputs:
- input_grad: bfloat16 [4, 192, 384, 192], P(None, 'lat', 'lon')
- qkv_weight_grad: float32 [192, 576], replicated
- out_weight_grad: float32 [192, 192], replicated
- gain_grad: float32 [192], replicated
- bias_grad: float32 [16, 2, 6, 20736], P('lat')
Inputs may be any that keep to these rules, and one draw needn't show every extreme that they name: `fields`: cells have a scale of their own and features a scale of their own.
All inputs are finite; a program needn't handle non-finite values.
Results may differ from a plain program's by a relative error of at most 0.0097.
Values may be sent and summed in bfloat16 or wider, within the bound.
A program may use at most 128 MiB of HBM per device.

v0:
```python
import jax
import jax.numpy as jnp
from jax import lax
from jax.sharding import PartitionSpec as P

WIN_LEVELS = 2
WIN_LAT = 12
WIN_LON = 6
WIN_TOKENS = 144


EPS = 1e-05
MASKED = -1e30


def from_behind(block, axis, distance):
    devices = range(lax.axis_size(axis))
    route = [(i - distance, i) for i in devices if i - distance in devices]
    return lax.ppermute(block, axis, route)


def shifted(value, axis, steps):
    count = lax.axis_size(axis)
    pairs = [(source, (source + steps) % count) for source in range(count)]
    return lax.ppermute(value, axis, pairs)


def to_windows(field, level_windows, lon_windows):
    levels, lat_rows, lon_cols, features = field.shape
    field = field.reshape(
        level_windows,
        levels // level_windows,
        lat_rows,
        lon_windows,
        lon_cols // lon_windows,
        features,
    )
    field = field.transpose(0, 3, 1, 2, 4, 5)
    return field.reshape(-1, features)


def from_windows(flat, levels, lat_rows, lon_cols, level_windows, lon_windows):
    features = flat.shape[1]
    field = flat.reshape(
        level_windows,
        lon_windows,
        levels // level_windows,
        lat_rows,
        lon_cols // lon_windows,
        features,
    )
    field = field.transpose(0, 2, 3, 1, 4, 5)
    return field.reshape(levels, lat_rows, lon_cols, features)


def window_row(normed_row, grad_row, bias_row, lat_group, qkv_weight, out_weight):
    levels, lat_rows, lon_cols, features = normed_row.shape
    level_windows = levels // WIN_LEVELS
    lon_windows = lon_cols // WIN_LON
    head_count = bias_row.shape[1]
    head_width = features // head_count
    score_scale = head_width ** (-0.5)
    position = jnp.arange(WIN_TOKENS)
    level_pos = position // (lat_rows * WIN_LON)
    lat_pos = position // WIN_LON % lat_rows
    token_group = jnp.sum(
        jnp.where(lat_pos[:, None] == jnp.arange(lat_rows)[None, :], lat_group[None, :], 0), axis=1
    )
    level_flag = jnp.arange(level_windows)[:, None] * WIN_LEVELS + level_pos[None, :] == levels - 1
    allowed = (
        (token_group[None, :, None] >= 0)
        & (token_group[None, :, None] == token_group[None, None, :])
        & (level_flag[:, :, None] == level_flag[:, None, :])
    )
    inputs = to_windows(normed_row, level_windows, lon_windows)
    upstream = to_windows(grad_row, level_windows, lon_windows)
    live = jnp.broadcast_to(token_group >= 0, (level_windows, lon_windows, WIN_TOKENS)).reshape(
        -1, 1
    )
    upstream = jnp.where(live, upstream, jnp.zeros_like(upstream))
    projected = jnp.dot(inputs, qkv_weight, preferred_element_type=jnp.float32)

    def split_heads(block):
        return block.astype(jnp.bfloat16).reshape(
            level_windows, lon_windows, WIN_TOKENS, head_count, head_width
        )

    query_heads = split_heads(projected[:, :features])
    key_heads = split_heads(projected[:, features : 2 * features])
    value_heads = split_heads(projected[:, 2 * features :])
    f32 = jnp.float32
    scores = (
        jnp.einsum("znqhd,znkhd->znhqk", query_heads, key_heads, preferred_element_type=f32)
        * score_scale
        + bias_row[:, None]
    )
    scores = jnp.where(allowed[:, None, None], scores, MASKED)
    row_max = jnp.max(scores, axis=-1, keepdims=True)
    exps = jnp.exp(scores - row_max)
    attention = exps / jnp.sum(exps, axis=-1, keepdims=True)
    attention_low = attention.astype(jnp.bfloat16)
    attended = (
        jnp.einsum("znhqk,znkhd->znqhd", attention_low, value_heads, preferred_element_type=f32)
        .astype(jnp.bfloat16)
        .reshape(-1, features)
    )
    out_part = jnp.dot(attended.T, upstream, preferred_element_type=f32)
    grad_attended = jnp.dot(upstream, out_weight.T, preferred_element_type=f32).astype(jnp.bfloat16)
    grad_attended = grad_attended.reshape(
        level_windows, lon_windows, WIN_TOKENS, head_count, head_width
    )
    grad_attention = jnp.einsum(
        "znqhd,znkhd->znhqk", grad_attended, value_heads, preferred_element_type=f32
    )
    grad_values = jnp.einsum(
        "znhqk,znqhd->znkhd", attention_low, grad_attended, preferred_element_type=f32
    ).astype(jnp.bfloat16)
    grad_scores = attention * (
        grad_attention - jnp.sum(attention * grad_attention, axis=-1, keepdims=True)
    )
    bias_part = jnp.sum(grad_scores, axis=1)
    grad_scores_low = grad_scores.astype(jnp.bfloat16)
    grad_queries = (
        jnp.einsum("znhqk,znkhd->znqhd", grad_scores_low, key_heads, preferred_element_type=f32)
        * score_scale
    ).astype(jnp.bfloat16)
    grad_keys = (
        jnp.einsum("znhqk,znqhd->znkhd", grad_scores_low, query_heads, preferred_element_type=f32)
        * score_scale
    ).astype(jnp.bfloat16)
    grad_projected = jnp.concatenate(
        [
            grad_queries.reshape(-1, features),
            grad_keys.reshape(-1, features),
            grad_values.reshape(-1, features),
        ],
        axis=1,
    )
    qkv_part = jnp.dot(inputs.T, grad_projected, preferred_element_type=f32)
    grad_inputs = jnp.dot(grad_projected, qkv_weight.T, preferred_element_type=f32).astype(
        jnp.bfloat16
    )
    grad_inputs = from_windows(grad_inputs, levels, lat_rows, lon_cols, level_windows, lon_windows)
    return (grad_inputs, qkv_part, out_part, bias_part)


def local(fields, out_grad, gain, qkv_weight, out_weight, window_bias):
    lat_count = lax.axis_size("lat")
    lat_index = lax.axis_index("lat")
    levels, lat_rows, lon_cols, features = fields.shape
    half_lat = WIN_LAT // 2
    half_lon = WIN_LON // 2
    win_count, level_windows, head_count = (
        window_bias.shape[0],
        window_bias.shape[1],
        window_bias.shape[2],
    )
    tables = window_bias.reshape(win_count, level_windows, head_count, WIN_TOKENS, WIN_TOKENS)
    values32 = fields.astype(jnp.float32)
    centred = values32 - jnp.mean(values32, axis=-1, keepdims=True)
    inv_std = lax.rsqrt(jnp.mean(centred * centred, axis=-1, keepdims=True) + EPS)
    standard = centred * inv_std
    normed = (standard * gain).astype(jnp.bfloat16)
    rolled_in = jnp.roll(normed, -1, axis=0)
    rolled_grad = jnp.roll(out_grad, -1, axis=0)
    keep_rows = lat_rows - half_lat
    tails = (rolled_in[:, keep_rows:], rolled_grad[:, keep_rows:])
    row_index = jnp.arange(lat_rows)
    above = from_behind((tails[0], tails[1]), "lat", 1)
    blank = jnp.zeros((levels, WIN_LAT - half_lat, lon_cols, features), jnp.bfloat16)
    block_in = jnp.concatenate([above[0], rolled_in[:, :keep_rows], tails[0], blank], axis=1)
    block_grad = jnp.concatenate([above[1], rolled_grad[:, :keep_rows], tails[1], blank], axis=1)
    main_group = jnp.where((row_index < half_lat) & (lat_index == 0), -1, 0)
    extra_index = jnp.arange(WIN_LAT)
    extra_group = jnp.where((extra_index < half_lat) & (lat_index == lat_count - 1), 0, -1)
    row_groups = jnp.concatenate([main_group, extra_group]).astype(jnp.int32)
    bias_rows = jnp.concatenate([tables, tables[win_count - 1 :]], axis=0)
    lefts = shifted((block_in[:, :, :half_lon], block_grad[:, :, :half_lon]), "lon", -1)
    shifted_in = jnp.concatenate([block_in[:, :, half_lon:], lefts[0]], axis=2)
    shifted_grad = jnp.concatenate([block_grad[:, :, half_lon:], lefts[1]], axis=2)
    row_count = shifted_in.shape[1] // WIN_LAT

    def stack_rows(field):
        return jnp.moveaxis(field.reshape(levels, row_count, WIN_LAT, lon_cols, features), 1, 0)

    def visit(carry, items):
        part_in, part_grad, part_bias, part_group = items
        grad_inputs, qkv_part, out_part, bias_part = window_row(
            part_in, part_grad, part_bias, part_group, qkv_weight, out_weight
        )
        return ((carry[0] + qkv_part, carry[1] + out_part), (grad_inputs, bias_part))

    start = (
        jnp.zeros((features, 3 * features), jnp.float32),
        jnp.zeros((features, features), jnp.float32),
    )
    (qkv_sum, out_sum), (grad_rows, bias_rows_grad) = lax.scan(
        visit,
        start,
        (
            stack_rows(shifted_in),
            stack_rows(shifted_grad),
            bias_rows,
            row_groups.reshape(row_count, WIN_LAT),
        ),
    )
    grad_shifted = jnp.moveaxis(grad_rows, 0, 1).reshape(
        levels, row_count * WIN_LAT, lon_cols, features
    )
    wrapped = shifted(grad_shifted[:, :, lon_cols - half_lon :], "lon", 1)
    grad_lon = jnp.concatenate([wrapped, grad_shifted[:, :, : lon_cols - half_lon]], axis=2)
    first_rows = grad_lon[:, :half_lat]
    below = from_behind(first_rows, "lat", -1)
    tail_grad = below + grad_lon[:, lat_rows : lat_rows + half_lat]
    bias_local = bias_rows_grad[:win_count].at[win_count - 1].add(bias_rows_grad[win_count])
    bias_flat = bias_local.reshape(win_count, level_windows, head_count, WIN_TOKENS * WIN_TOKENS)
    grad_normed = jnp.concatenate([grad_lon[:, half_lat:lat_rows], tail_grad], axis=1)
    grad_normed = jnp.roll(grad_normed, 1, axis=0)
    grad32 = grad_normed.astype(jnp.float32)
    gain_part = jnp.sum(grad32 * standard, axis=(0, 1, 2))
    scaled = grad32 * gain
    input_grad = out_grad.astype(jnp.float32) + inv_std * (
        scaled
        - jnp.mean(scaled, axis=-1, keepdims=True)
        - standard * jnp.mean(scaled * standard, axis=-1, keepdims=True)
    )
    qkv_total, out_total, gain_total = lax.psum((qkv_sum, out_sum, gain_part), ("lat", "lon"))
    bias_total = lax.psum(bias_flat, "lon")
    return (input_grad.astype(jnp.bfloat16), qkv_total, out_total, gain_total, bias_total)


def solution(mesh):
    in_specs = (
        P(None, "lat", "lon", None),
        P(None, "lat", "lon", None),
        P(),
        P(),
        P(),
        P("lat", None, None, None),
    )
    out_specs = (P(None, "lat", "lon", None), P(), P(), P(), P("lat", None, None, None))
    return jax.shard_map(local, mesh=mesh, in_specs=in_specs, out_specs=out_specs, check_vma=False)
```

profile of v0, /device:TPU:1, one launch (start us, length us, event | category | flops | bytes accessed | tf_op | source)
XLA Modules:
  0.0 730.1 jit_solution(6420198469655351831)
XLA Ops:
  8.9 2.0 fusion.55
  14.1 4.7 collective-permute-start
  19.7 3.2 collective-permute-start.2
  22.9 4.3 reshape.361
  27.3 2.2 slice.133
  29.5 3.6 slice.134
  33.2 4.4 pad_maximum_fusion
  42.3 5.7 collective-permute-start.1
  51.9 182.9 %while.21 = (s32[]{:T(128)}, f32[192,576]{1,0:T(8,128)}, f32[192,192]{1,0:T(8,128)}, bf16[3,4,12,12,192]{4,1,3,2,0:T(4,128)(2,1)}, f32[3,2,6,144,144]{3,4,2,1,0:...) while((s32[]{:T(128)}, f32[192,576]{1,0:T(8,128)}, ...), condition=%wide.region_8.9_spmd.clone, body=%wide.region_2.8_spmd.clone.sunk | while | flops 668317376 | bytes 61458148 | solution.py:197
  52.9 2.0 constant_dynamic-slice_fusion.6
  61.4 1.9 copy.186
  63.4 3.9 fusion.131
  67.2 2.2 reshape.395
  72.0 2.0 reshape.402
  74.3 1.9 reshape.396
  78.3 1.9 select_n.122
  80.2 2.0 convolution_add_fusion.5
  86.0 2.0 convolution_convert_fusion.9
  88.0 2.0 reshape.398
  92.9 2.0 reshape.401
  94.9 1.9 multiply_reduce_fusion.2
  96.8 3.3 fusion.132
  102.0 2.0 reshape.400
  113.2 2.0 constant_dynamic-slice_fusion.6
  121.7 1.9 copy.186
  123.6 3.9 fusion.131
  127.5 2.2 reshape.395
  132.2 2.0 reshape.402
  134.5 1.9 reshape.396
  140.4 2.1 convolution_add_fusion.5
  146.3 2.0 convolution_convert_fusion.9
  148.3 2.0 reshape.398
  153.1 2.0 reshape.401
  155.2 1.9 multiply_reduce_fusion.2
  157.1 3.3 fusion.132
  162.3 2.0 reshape.400
  169.8 2.3 convolution_add_fusion.4
  174.5 2.0 constant_dynamic-slice_fusion.6
  183.0 1.9 copy.186
  184.9 3.9 fusion.131
  188.8 2.2 reshape.395
  193.5 2.0 reshape.402
  195.8 1.9 reshape.396
  199.8 1.9 select_n.122
  201.7 2.1 convolution_add_fusion.5
  207.6 2.0 convolution_convert_fusion.9
  209.6 2.0 reshape.398
  214.4 2.0 reshape.401
  216.5 1.9 multiply_reduce_fusion.2
  218.4 3.3 fusion.132
  223.6 2.0 reshape.400
  231.1 2.3 convolution_add_fusion.4
  234.8 2.3 slice.147
  237.2 2.2 add_dynamic-update-slice_fusion
  239.4 3.4 copy.112
  242.8 5.3 reshape.364
  249.7 3.1 collective-permute-done.4
  254.7 4.7 collective-permute-done.5
  260.1 2.5 fusion.57
  262.7 2.0 fusion.54
  265.6 83.7 %psum.30 = f32[192]{0:T(256)} all-reduce(f32[192]{0:T(256)S(1)} %get-tuple-element.285), channel_id=1, replica_groups=mesh['lat'=8,'lon'=32] {'lat','lon'}, use_global_device_ids=true, to_apply=%region_14.15 | all-reduce | flops 192 | bytes 1536 | tf_op jit(solution)/shard_map/psum | solution.py:227
  349.3 138.6 %all-reduce.6.cloned.1.call-done = (f32[192,576]{1,0:T(8,128)}, f32[192,192]{1,0:T(8,128)}) async-done(((f32[192,576]{1,0:T(8,128)}, f32[192,192]{1,0:T(8,128)}), (f32[192,576]{1,0:T(8,128)}, f32[192,192]{1,0:T(8,128)})) %all-reduce.6.cloned.1.call-update) | async-done | bytes 589840 | tf_op jit(solution)/shard_map/psum | solution.py:227
  487.9 228.9 %all-reduce.4.cloned.1.call-done = f32[2,2,6,20736]{3,1,2,0:T(2,128)} async-done(((f32[2,2,6,20736]{3,1,2,0:T(2,128)}), f32[2,2,6,20736]{3,1,2,0:T(2,128)}) %all-reduce.4.cloned.1.call-update) | async-done | bytes 1990672 | tf_op jit(solution)/shard_map/psum | solution.py:228
  720.3 3.0 copy.221
  (285 shorter events, 109.0 us)
Async XLA Ops:
  7.2 4.5 copy-start.6
  7.2 4.5 copy-start.26
  7.2 480.7 %all-reduce.6.cloned.1.call-start = ((), (), s32[]{:S(2)}) async-start(), calls=%async_computation.1 | async-start | bytes 1376256 | tf_op jit(solution)/shard_map/psum | solution.py:227
  8.9 4.1 copy-start.10
  11.0 0.7 copy-start.14
  12.7 6.1 copy-start.18
  13.0 6.7 copy-start.8
  13.2 9.7 %copy-start.16 = (bf16[1,24,12,192]{3,0,2,1:T(2,128)(2,1)}, bf16[1,24,12,192]{3,0,2,1:T(2,128)(2,1)S(1)}, u32[]{:S(2)}) copy-start(bf16[1,24,12,192]{3,0,2,1:T(2,128)(2,1)S(1)} %slice.157) | copy-start | bytes 331780
  14.1 26.3 %collective-permute-start = (bf16[4,6,12,192]{3,0,2,1:T(4,128)(2,1)}, bf16[4,6,12,192]{3,0,2,1:T(4,128)(2,1)}, u32[]{:S(2)}, u32[]{:S(2)}) collective-permute-start(bf16[4,6,12,192]{3,0,2,1:T(4,128)(2,1)} %pad_maximum_fusion.6), channel_id=1, source_target_pairs={{0,32},{32,64},{64,96},{96,128},{128,160},{160,192},{192,224},{1,3... | collective-permute-start | bytes 331784 | tf_op jit(solution)/shard_map/ppermute | solution.py:19
  18.8 4.1 copy-start.12
  18.8 4.1 copy-start.20
  19.7 17.9 %collective-permute-start.2 = (bf16[4,6,12,192]{3,1,2,0:T(8,128)(2,1)}, bf16[4,6,12,192]{3,1,2,0:T(8,128)(2,1)}, u32[]{:S(2)}, u32[]{:S(2)}) collective-permute-start(bf16[4,6,12,192]{3,1,2,0:T(8,128)(2,1)} %pad_maximum_fusion.4), channel_id=1, source_target_pairs={{0,32},{32,64},{64,96},{96,128},{128,160},{160,192},{192,224},{1,3... | collective-permute-start | bytes 331784 | tf_op jit(solution)/shard_map/ppermute | solution.py:19
  33.2 4.4 copy-start.13
  33.2 4.4 copy-start.21
  37.6 2.8 copy-start.9
  37.6 2.8 copy-start.17
  39.0 9.4 %collective-permute-start.3 = (bf16[4,36,3,192]{3,1,2,0:T(8,128)(2,1)S(1)}, bf16[4,36,3,192]{3,1,2,0:T(8,128)(2,1)S(1)}, u32[]{:S(2)}, u32[]{:S(2)}) collective-permute-start(bf16[4,36,3,192]{3,1,2,0:T(8,128)(2,1)S(1)} %slice.161), channel_id=1, source_target_pairs={{0,31},{1,0},{2,1},{3,2},{4,3},{5,4},{6,5},{7,6},{8,7},{9,8},{10,9... | collective-permute-start | bytes 497672 | tf_op jit(solution)/shard_map/ppermute | solution.py:25
  42.3 8.1 %collective-permute-start.1 = (bf16[4,36,3,192]{3,0,2,1:T(4,128)(2,1)S(1)}, bf16[4,36,3,192]{3,0,2,1:T(4,128)(2,1)S(1)}, u32[]{:S(2)}, u32[]{:S(2)}) collective-permute-start(bf16[4,36,3,192]{3,0,2,1:T(4,128)(2,1)S(1)} %slice.159), channel_id=1, source_target_pairs={{0,31},{1,0},{2,1},{3,2},{4,3},{5,4},{6,5},{7,6},{8,7},{9,8},{10,9... | collective-permute-start | bytes 497672 | tf_op jit(solution)/shard_map/ppermute | solution.py:25
  51.9 5.0 copy-start.28
  52.0 22.0 %copy-start.24 = (pred[144]{0:T(512)(128)(4,1)}, pred[144]{0:T(512)(128)(4,1)S(1)}, u32[]{:S(2)}) copy-start(pred[144]{0:T(512)(128)(4,1)S(1)} %broadcast_compare_fusion.2) | copy-start | bytes 436 | tf_op jit(solution)/shard_map/while
  55.4 4.3 copy-start.1
  67.2 27.6 %copy-start = (f32[2,2,6,144,144]{3,4,2,1,0:T(8,128)}, f32[2,2,6,144,144]{3,4,2,1,0:T(8,128)S(1)}, u32[]{:S(2)}) copy-start(f32[2,2,6,144,144]{3,4,2,1,0:T(8,128)S(1)} %get-tuple-element.413) | copy-start | bytes 5971972 | tf_op jit(solution)/shard_map/while
  74.3 7.9 %copy-start.25 = (pred[144]{0:T(512)(128)(4,1)S(1)}, pred[144]{0:T(512)(128)(4,1)}, u32[]{:S(2)}) copy-start(pred[144]{0:T(512)(128)(4,1)} %copy-done.24) | copy-start | bytes 436 | tf_op jit(solution)/shard_map/while
  94.9 1.9 copy-start.23
  96.8 3.3 copy-start.3
  105.4 1.0 copy-start.5
  105.4 1.1 copy-start.4
  107.8 1.7 copy-start.2
  110.7 1.4 copy-start.29
  112.1 5.0 copy-start.28
  112.2 22.0 %copy-start.24 = (pred[144]{0:T(512)(128)(4,1)}, pred[144]{0:T(512)(128)(4,1)S(1)}, u32[]{:S(2)}) copy-start(pred[144]{0:T(512)(128)(4,1)S(1)} %broadcast_compare_fusion.2) | copy-start | bytes 436 | tf_op jit(solution)/shard_map/while
  115.6 4.3 copy-start.1
  127.5 27.7 %copy-start = (f32[2,2,6,144,144]{3,4,2,1,0:T(8,128)}, f32[2,2,6,144,144]{3,4,2,1,0:T(8,128)S(1)}, u32[]{:S(2)}) copy-start(f32[2,2,6,144,144]{3,4,2,1,0:T(8,128)S(1)} %get-tuple-element.413) | copy-start | bytes 5971972 | tf_op jit(solution)/shard_map/while
  134.5 8.0 %copy-start.25 = (pred[144]{0:T(512)(128)(4,1)S(1)}, pred[144]{0:T(512)(128)(4,1)}, u32[]{:S(2)}) copy-start(pred[144]{0:T(512)(128)(4,1)} %copy-done.24) | copy-start | bytes 436 | tf_op jit(solution)/shard_map/while
  155.2 1.9 copy-start.23
  157.1 3.3 copy-start.3
  165.6 1.0 copy-start.5
  165.6 1.1 copy-start.4
  168.1 1.7 copy-start.2
  172.0 1.4 copy-start.29
  173.4 5.0 copy-start.28
  173.5 22.0 %copy-start.24 = (pred[144]{0:T(512)(128)(4,1)}, pred[144]{0:T(512)(128)(4,1)S(1)}, u32[]{:S(2)}) copy-start(pred[144]{0:T(512)(128)(4,1)S(1)} %broadcast_compare_fusion.2) | copy-start | bytes 436 | tf_op jit(solution)/shard_map/while
  176.9 4.3 copy-start.1
  188.8 27.7 %copy-start = (f32[2,2,6,144,144]{3,4,2,1,0:T(8,128)}, f32[2,2,6,144,144]{3,4,2,1,0:T(8,128)S(1)}, u32[]{:S(2)}) copy-start(f32[2,2,6,144,144]{3,4,2,1,0:T(8,128)S(1)} %get-tuple-element.413) | copy-start | bytes 5971972 | tf_op jit(solution)/shard_map/while
  195.8 8.0 %copy-start.25 = (pred[144]{0:T(512)(128)(4,1)S(1)}, pred[144]{0:T(512)(128)(4,1)}, u32[]{:S(2)}) copy-start(pred[144]{0:T(512)(128)(4,1)} %copy-done.24) | copy-start | bytes 436 | tf_op jit(solution)/shard_map/while
  216.5 1.9 copy-start.23
  218.4 3.3 copy-start.3
  226.9 1.0 copy-start.5
  226.9 1.1 copy-start.4
  229.4 1.8 copy-start.2
  233.4 1.4 copy-start.29
  237.1 479.7 %all-reduce.4.cloned.1.call-start = ((), (), s32[]{:S(2)}) async-start(), calls=%async_computation | async-start | bytes 3981312 | tf_op jit(solution)/shard_map/psum | solution.py:228
  248.1 1.2 copy-start.22
  249.4 3.4 collective-permute-start.4
  252.9 7.2 copy-start.7
  252.9 7.2 copy-start.11
  252.9 7.2 copy-start.15
  252.9 7.2 copy-start.27
  252.9 6.4 collective-permute-start.5
  260.1 2.5 copy-start.19
Sparse Core Ops, SparseCore 0:
  237.3 250.6 all-reduce.5
  491.3 225.4 all-reduce.3
where the time goes:
time: 734 us; the launch traced here: 730 us
  waiting for transfers between devices  375 us (51%)
  local copies, waits for them, and re-layouts  140 us (19%)
  blocking collectives  83.7 us (11%)
  matrix products  59 us (8%)
  other arithmetic  40.6 us (6%)
  starting transfers between devices  16.6 us (2%)
  between operations  14.4 us (2%)
    psum x1, waiting for transfers between devices, local(): bias_total = lax.psum(bias_flat, 'lon')  229 us
    psum x1, waiting for transfers between devices, local(): lax.psum((qkv_sum, out_sum, gain_part), ('lat', 'lon'))  139 us
    psum x1, blocking collectives, local(): lax.psum((qkv_sum, out_sum, gain_part), ('lat', 'lon'))  83.7 us
    dynamic_slice x9, local copies, waits for them, and re-layouts, local(): lax.scan(visit, start, (stack_rows(shifted_in), stack_rows(shifted_grad),...  16.8 us
  transfers between devices with their start and end apart: 8, of which 4 were waited for; matrix products, arithmetic and copies ran while one was open for 5% of the time, Pallas kernels for 0%

commit v1 on v0

v1 whole, which is shorter than its diff:
```python
import jax
import jax.numpy as jnp
from jax import lax
from jax.experimental import pallas as pl
from jax.experimental.pallas import tpu as pltpu
from jax.sharding import PartitionSpec as P

F32 = jnp.float32
BF16 = jnp.bfloat16
MESH = pl.DeviceIdType.MESH

EPS = 1e-05
MASKED = -1e30

LEVELS = 4
ROWS = 24
COLS = 12
WIDTH = 192
HEADS = 6
HEAD = 32
TOKENS = 144
HALF = 72
LATS = 8
LONS = 32
Z = 8

BIAS_ROWS = 96
WEIGHT_ROWS = 48
SHARD = BIAS_ROWS + WEIGHT_ROWS
BIAS_ALL = LONS * BIAS_ROWS

VMEM_LIMIT = 56 * 1024 * 1024


def vmem_spec():
    return pl.BlockSpec(memory_space=pltpu.VMEM)


def params(**kw):
    return pltpu.CompilerParams(vmem_limit_bytes=VMEM_LIMIT, **kw)


def pack_in_kernel(fields_ref, grad_ref, a_ref, b_ref, tmp_ref):
    for k, ref in enumerate((fields_ref, grad_ref)):
        for r in range(6):
            for lev in range(LEVELS):
                at = r * 48 + lev * 12
                tmp_ref[at : at + 12, :] = ref[lev, 18 + r].astype(F32)
        a_ref[k] = tmp_ref[...].astype(BF16)
    for k, ref in enumerate((fields_ref, grad_ref)):
        for r in range(ROWS):
            for lev in range(LEVELS):
                at = ((r - 18) % ROWS) * 12 + lev * 3
                tmp_ref[at : at + 3, :] = ref[lev, r].astype(F32)[0:3]
        b_ref[k] = tmp_ref[...].astype(BF16)


def pack_in(fields, grad):
    shape = jax.ShapeDtypeStruct((2, 288, WIDTH), BF16)
    return pl.pallas_call(
        pack_in_kernel,
        out_shape=(shape, shape),
        in_specs=[vmem_spec()] * 2,
        out_specs=(vmem_spec(), vmem_spec()),
        scratch_shapes=[pltpu.VMEM((288, WIDTH), F32)],
        compiler_params=params(),
        name="pack_in",
    )(fields, grad)


def halo_kernel(step, a_ref, b_ref, ra_ref, rb_ref, rc_ref, send, recv):
    lat = lax.axis_index("lat")
    lon = lax.axis_index("lon")
    to_lat = (lat + step + LATS) % LATS
    to_lon = (lon - step + LONS) % LONS
    from_lat = (lat - step + LATS) % LATS
    from_lon = (lon + step + LONS) % LONS
    barrier = pltpu.get_barrier_semaphore()
    for there in ((from_lat, lon), (lat, from_lon), (from_lat, from_lon)):
        pl.semaphore_signal(barrier, inc=1, device_id=there, device_id_type=MESH)
    pl.semaphore_wait(barrier, 3)
    plan = (
        (a_ref, ra_ref, (to_lat, lon)),
        (b_ref, rb_ref, (lat, to_lon)),
        (b_ref.at[:, 0:80], rc_ref, (to_lat, to_lon)),
    )
    copies = [
        pltpu.make_async_remote_copy(
            src_ref=source,
            dst_ref=target,
            send_sem=send.at[k],
            recv_sem=recv.at[k],
            device_id=there,
            device_id_type=MESH,
        )
        for k, (source, target, there) in enumerate(plan)
    ]
    for copy in copies:
        copy.start()
    for copy in copies:
        copy.wait()


def halo(step, a, b):
    return pl.pallas_call(
        lambda *refs: halo_kernel(step, *refs),
        out_shape=(
            jax.ShapeDtypeStruct(a.shape, BF16),
            jax.ShapeDtypeStruct(b.shape, BF16),
            jax.ShapeDtypeStruct((b.shape[0], 80, WIDTH), BF16),
        ),
        in_specs=[vmem_spec()] * 2,
        out_specs=(vmem_spec(),) * 3,
        scratch_shapes=[pltpu.SemaphoreType.DMA((3,)), pltpu.SemaphoreType.DMA((3,))],
        compiler_params=params(collective_id=0 if step == 1 else 1, has_side_effects=True),
        name="halo",
    )(a, b)


def assemble_kernel(fields_ref, grad_ref, a_ref, b_ref, c_ref, xw_ref, gw_ref, tmp_ref, b32_ref, c32_ref):
    lat = lax.axis_index("lat")
    for k, (own, out) in enumerate(((fields_ref, xw_ref), (grad_ref, gw_ref))):
        b32_ref[...] = b_ref[k].astype(F32)
        c32_ref[...] = c_ref[k].astype(F32)
        for w in range(2):
            for g in range(3):
                for zl in range(2):
                    lev = (2 * w + zl + 1) % LEVELS
                    for lp in range(12):
                        at = (zl * 12 + lp) * 6
                        row = 12 * g + lp - 6
                        if row >= ROWS:
                            tmp_ref[0, at : at + 6, :] = jnp.zeros((6, WIDTH), F32)
                            tmp_ref[1, at : at + 6, :] = jnp.zeros((6, WIDTH), F32)
                            continue
                        if row < 0:
                            from_a = (row + 6) * 48 + lev * 12
                            tile = a_ref[k, from_a : from_a + 12, :].astype(F32)
                            from_c = (row + 6) * 12 + lev * 3
                            east = c32_ref[from_c : from_c + 3, :]
                            tile = jnp.where(lat == 0, 0.0, tile)
                            east = jnp.where(lat == 0, 0.0, east)
                        else:
                            tile = own[lev, row].astype(F32)
                            from_b = ((row - 18) % ROWS) * 12 + lev * 3
                            east = b32_ref[from_b : from_b + 3, :]
                        tmp_ref[0, at : at + 6, :] = tile[3:9]
                        tmp_ref[1, at : at + 3, :] = tile[9:12]
                        tmp_ref[1, at + 3 : at + 6, :] = east
                out[w, g] = tmp_ref[...].astype(BF16)


def assemble(fields, grad, a, b, c):
    shape = jax.ShapeDtypeStruct((2, 3, 2, TOKENS, WIDTH), BF16)
    return pl.pallas_call(
        assemble_kernel,
        out_shape=(shape, shape),
        in_specs=[vmem_spec()] * 5,
        out_specs=(vmem_spec(), vmem_spec()),
        scratch_shapes=[
            pltpu.VMEM((2, TOKENS, WIDTH), F32),
            pltpu.VMEM((288, WIDTH), F32),
            pltpu.VMEM((80, WIDTH), F32),
        ],
        compiler_params=params(),
        name="assemble",
    )(fields, grad, a, b, c)


def dot(a, b, contract=(1, 0)):
    return lax.dot_general(
        a, b, (((contract[0],), (contract[1],)), ((), ())), preferred_element_type=F32
    )


def window(n, x_ref, g_ref, gain, qkv_ref, qkv_t_ref, out_ref, bias_ref, first, bias_acc, weight_acc, gain_acc, ig_ref):
    scale = HEAD ** (-0.5)
    x = x_ref[n].astype(F32)
    centred = x - jnp.mean(x, axis=-1, keepdims=True)
    inv_std = lax.rsqrt(jnp.mean(centred * centred, axis=-1, keepdims=True) + EPS)
    standard = centred * inv_std
    normed = (standard * gain).astype(BF16)
    upstream = g_ref[n]
    projected = dot(normed, qkv_ref[...]).astype(BF16)
    projected_t = dot(qkv_t_ref[...], normed, (1, 1)).astype(BF16)
    attended_grad = dot(upstream, out_ref[...], (1, 1)).astype(BF16)
    attended_grad_t = dot(out_ref[...], upstream, (1, 1)).astype(BF16)
    lane = lax.broadcasted_iota(jnp.int32, (TOKENS, 128), 1)
    attended_parts, queries_parts, keys_parts, values_parts = [], [], [], []
    for h in range(HEADS):
        lo = 128 * (h // 4)
        width = 128 if h < 4 else 64
        own = (lane[:, :width] // HEAD) == (h % 4)
        queries = jnp.where(own, projected[:, lo : lo + width], jnp.zeros((), BF16))
        keys = projected[:, WIDTH + lo : WIDTH + lo + width]
        values = projected[:, 2 * WIDTH + lo : 2 * WIDTH + lo + width]
        upper = jnp.where(own, attended_grad[:, lo : lo + width], jnp.zeros((), BF16))
        rows = slice(h * HEAD, (h + 1) * HEAD)
        queries_t = projected_t[h * HEAD : (h + 1) * HEAD]
        keys_t = projected_t[WIDTH + h * HEAD : WIDTH + (h + 1) * HEAD]
        values_t = projected_t[2 * WIDTH + h * HEAD : 2 * WIDTH + (h + 1) * HEAD]
        scores = dot(queries, keys, (1, 1)) * scale + bias_ref[h]
        exps = jnp.exp(scores - jnp.max(scores, axis=-1, keepdims=True))
        attention = exps * (1.0 / jnp.sum(exps, axis=-1, keepdims=True))
        low = attention.astype(BF16)
        attention_grad = dot(upper, values, (1, 1))
        delta = jnp.sum(attention * attention_grad, axis=-1, keepdims=True)
        scores_grad = attention * (attention_grad - delta)
        if n == 0:
            @pl.when(first)
            def _():
                bias_acc[h] = scores_grad

            @pl.when(jnp.logical_not(first))
            def _():
                bias_acc[h] += scores_grad
        else:
            bias_acc[h] += scores_grad
        scores_low = scores_grad.astype(BF16)
        attended_parts.append(dot(values_t, low, (1, 1)).astype(BF16))
        values_parts.append(dot(attended_grad_t[rows], low).astype(BF16))
        queries_parts.append((dot(keys_t, scores_low, (1, 1)) * scale).astype(BF16))
        keys_parts.append((dot(queries_t, scores_low) * scale).astype(BF16))
    attended_t = jnp.concatenate(attended_parts, axis=0)
    projected_grad_t = jnp.concatenate(queries_parts + keys_parts + values_parts, axis=0)
    weight_acc[3 * WIDTH :, :] += dot(attended_t, upstream)
    weight_acc[: 3 * WIDTH, :] += dot(projected_grad_t, normed)
    shifted_t = dot(qkv_ref[...], projected_grad_t)
    grad = jnp.transpose(shifted_t).astype(BF16).astype(F32)
    product = grad * standard
    gain_acc[...] += jnp.sum(product, axis=0, keepdims=True)
    scaled = grad * gain
    ig = upstream.astype(F32) + inv_std * (
        scaled
        - jnp.mean(scaled, axis=-1, keepdims=True)
        - standard * jnp.mean(product * gain, axis=-1, keepdims=True)
    )
    ig_ref[n] = ig.astype(BF16)


def compute_kernel(
    x_ref, g_ref, gain_ref, qkv_ref, qkv_t_ref, out_ref, bias_ref,
    ig_ref, packed_ref, masked, bias_acc, weight_acc, gain_acc, flat,
):
    w, g = pl.program_id(0), pl.program_id(1)
    lat = lax.axis_index("lat")

    @pl.when((w == 0) & (g == 0))
    def _():
        weight_acc[...] = jnp.zeros_like(weight_acc)
        gain_acc[...] = jnp.zeros_like(gain_acc)
        flat[BIAS_ALL - 48 :, :] = jnp.zeros((48, 128), F32)

    @pl.when((g < 2) | (lat == LATS - 1))
    def _():
        q = lax.broadcasted_iota(jnp.int32, (TOKENS, TOKENS), 0)
        k = lax.broadcasted_iota(jnp.int32, (TOKENS, TOKENS), 1)
        half = ((q >= HALF) != (k >= HALF)) & (w == 1)
        q_low = ((q // 6) % 12) < 6
        k_low = ((k // 6) % 12) < 6
        top = (q_low | k_low) & (g == 0) & (lat == 0)
        bottom = jnp.logical_not(q_low & k_low) & (g == 2)
        blocked = half | top | bottom
        for h in range(HEADS):
            masked[h] = jnp.where(blocked, MASKED, bias_ref[0, 0, h])
        gain = gain_ref[...]
        for n in range(2):
            window(
                n, x_ref.at[0, 0], g_ref.at[0, 0], gain, qkv_ref, qkv_t_ref, out_ref, masked, g < 2,
                bias_acc, weight_acc, gain_acc, ig_ref.at[0, 0],
            )

    def fold(at, rows, take):
        tails = []
        for h in range(HEADS):
            value = take(h)
            flat[pl.ds(at + h * rows, rows), :] = value[:, :128]
            tails.append(value[:, 128:])
        tails.append(jnp.zeros((rows, 32), F32))
        flat[pl.ds(at + HEADS * rows, rows), :] = jnp.concatenate(tails, axis=1)

    for which in range(2):
        @pl.when((g == (0, 2)[which]) & (w == 0))
        def _():
            fold(which * 1512, TOKENS, lambda h: bias_acc[h])

        @pl.when((g == (0, 2)[which]) & (w == 1))
        def _():
            fold(which * 1512 + 1008, HALF, lambda h: bias_acc[h, :HALF, :] + bias_acc[h, HALF:, :])

    @pl.when((w == 1) & (g == 2))
    def _():
        zero = jnp.zeros((WEIGHT_ROWS, 128), BF16)
        for s in range(LONS):
            packed_ref[s, :BIAS_ROWS, :] = flat[s * BIAS_ROWS : (s + 1) * BIAS_ROWS, :].astype(BF16)
        for s in range(16):
            packed_ref[s, BIAS_ROWS:, :] = weight_acc[s * 48 : (s + 1) * 48, :128].astype(BF16)
        for s in range(8):
            pair = jnp.concatenate(
                [weight_acc[s * 48 : (s + 1) * 48, 128:], weight_acc[384 + s * 48 : 384 + (s + 1) * 48, 128:]],
                axis=1,
            )
            packed_ref[16 + s, BIAS_ROWS:, :] = pair.astype(BF16)
        total = gain_acc[...]
        left = jnp.broadcast_to(total[:, :128], (WEIGHT_ROWS, 128))
        right = jnp.concatenate([total[:, 128:], jnp.zeros((1, 64), F32)], axis=1)
        right = jnp.broadcast_to(right, (WEIGHT_ROWS, 128))
        row = lax.broadcasted_iota(jnp.int32, (WEIGHT_ROWS, 128), 0)
        packed_ref[24, BIAS_ROWS:, :] = jnp.where(row == 0, left, jnp.where(row == 1, right, 0.0)).astype(BF16)
        for s in range(25, LONS):
            packed_ref[s, BIAS_ROWS:, :] = zero


def compute(xw, gw, gain, qkv, out_weight, bias):
    whole = lambda *shape: pl.BlockSpec(shape, lambda w, g: (0,) * len(shape))
    window_spec = pl.BlockSpec((1, 1, 2, TOKENS, WIDTH), lambda w, g: (w, g, 0, 0, 0))
    return pl.pallas_call(
        compute_kernel,
        grid=(2, 3),
        out_shape=(
            jax.ShapeDtypeStruct((2, 3, 2, TOKENS, WIDTH), BF16),
            jax.ShapeDtypeStruct((LONS, SHARD, 128), BF16),
        ),
        in_specs=[
            window_spec,
            window_spec,
            whole(1, WIDTH),
            whole(WIDTH, 3 * WIDTH),
            whole(3 * WIDTH, WIDTH),
            whole(WIDTH, WIDTH),
            pl.BlockSpec((1, 1, HEADS, TOKENS, TOKENS), lambda w, g: (jnp.minimum(g, 1), w, 0, 0, 0)),
        ],
        out_specs=(window_spec, whole(LONS, SHARD, 128)),
        scratch_shapes=[
            pltpu.VMEM((HEADS, TOKENS, TOKENS), F32),
            pltpu.VMEM((HEADS, TOKENS, TOKENS), F32),
            pltpu.VMEM((4 * WIDTH, WIDTH), F32),
            pltpu.VMEM((1, WIDTH), F32),
            pltpu.VMEM((BIAS_ALL, 128), F32),
        ],
        compiler_params=params(),
        name="windows",
    )(xw, gw, gain.reshape(1, WIDTH), qkv, qkv.T, out_weight, bias)


def pack_out_kernel(ig_ref, tile_ref, e_ref, d_ref, w32_ref, tmp_ref):
    for w in range(2):
        for g in range(3):
            w32_ref[...] = ig_ref[w, g].astype(F32)
            for zl in range(2):
                lev = (2 * w + zl + 1) % LEVELS
                for lp in range(12 if g < 2 else 6):
                    at = (zl * 12 + lp) * 6
                    row = 12 * g + lp - 6
                    tile_ref[lev, row + 6, 3:9, :] = w32_ref[0, at : at + 6, :]
                    tile_ref[lev, row + 6, 9:12, :] = w32_ref[1, at : at + 3, :]
                    tile_ref[lev, row + 6, 0:3, :] = w32_ref[1, at + 3 : at + 6, :]
    for r in range(6):
        for lev in range(LEVELS):
            tmp_ref[r * 48 + lev * 12 : r * 48 + lev * 12 + 12, :] = tile_ref[lev, r]
    e_ref[0] = tmp_ref[:288, :].astype(BF16)
    for r in range(30):
        for lev in range(LEVELS):
            at = r * 12 + lev * 3
            tmp_ref[at : at + 3, :] = tile_ref[lev, r, 0:3, :]
    tmp_ref[360:, :] = jnp.zeros((8, WIDTH), F32)
    d_ref[0] = tmp_ref[...].astype(BF16)


def pack_out(ig):
    return pl.pallas_call(
        pack_out_kernel,
        out_shape=(
            jax.ShapeDtypeStruct((LEVELS, 30, COLS, WIDTH), F32),
            jax.ShapeDtypeStruct((1, 288, WIDTH), BF16),
            jax.ShapeDtypeStruct((1, 368, WIDTH), BF16),
        ),
        in_specs=[vmem_spec()],
        out_specs=(vmem_spec(),) * 3,
        scratch_shapes=[pltpu.VMEM((2, TOKENS, WIDTH), F32), pltpu.VMEM((368, WIDTH), F32)],
        compiler_params=params(),
        name="pack_out",
    )(ig)


def place_kernel(tile_ref, e_ref, d_ref, f_ref, out_ref, d32_ref, f32_ref):
    last = lax.axis_index("lat") == LATS - 1
    d32_ref[...] = d_ref[0].astype(F32)
    f32_ref[...] = f_ref[0].astype(F32)
    column = lax.broadcasted_iota(jnp.int32, (COLS, WIDTH), 0)
    for lev in range(LEVELS):
        for row in range(ROWS):
            if row < 18:
                own = tile_ref[lev, row + 6]
                at = (row + 6) * 12 + lev * 3
                west = d32_ref[at : at + 3, :]
            else:
                r = row - 18
                at = r * 48 + lev * 12
                own = jnp.where(last, tile_ref[lev, 24 + r], e_ref[0, at : at + 12, :].astype(F32))
                at = r * 12 + lev * 3
                west = jnp.where(last, d32_ref[288 + at : 288 + at + 3, :], f32_ref[at : at + 3, :])
            west = jnp.concatenate([west, jnp.zeros((COLS - 3, WIDTH), F32)], axis=0)
            out_ref[lev, row] = jnp.where(column < 3, west, own).astype(BF16)


def place(tiles, e, d, f):
    return pl.pallas_call(
        place_kernel,
        out_shape=jax.ShapeDtypeStruct((LEVELS, ROWS, COLS, WIDTH), BF16),
        in_specs=[vmem_spec()] * 4,
        out_specs=vmem_spec(),
        scratch_shapes=[pltpu.VMEM((368, WIDTH), F32), pltpu.VMEM((80, WIDTH), F32)],
        compiler_params=params(),
        name="place",
    )(tiles, e, d, f)


def sums_kernel(
    src, out, core_buf, x_buf, z_buf, lat_buf, held, weights,
    core_send, core_recv, x_send, x_recv, z_send, z_recv, lat_send, lat_recv,
    gz_send, gz_recv, gw_send, gw_recv, gx_send, gx_recv, gc_send, gc_recv,
):
    lat = lax.axis_index("lat")
    lon = lax.axis_index("lon")
    z, x, core = lon // 4, (lon // 2) % 2, lon % 2

    def at_lon(zz, xx, cc):
        return (lat, zz * 4 + xx * 2 + cc)

    core_peer = at_lon(z, x, 1 - core)
    x_peer = at_lon(z, 1 - x, core)
    z_peers = [at_lon((z + d) % Z, x, core) for d in range(1, Z)]
    lat_peers = [((lat + d) % LATS, lon) for d in range(1, LATS)]
    barrier = pltpu.get_barrier_semaphore()
    for there in [core_peer, x_peer] + z_peers + lat_peers:
        pl.semaphore_signal(barrier, inc=1, device_id=there, device_id_type=MESH)
    pl.semaphore_wait(barrier, 2 + 2 * (Z - 1))

    def copy(source, target, send, recv, there):
        return pltpu.make_async_remote_copy(
            src_ref=source, dst_ref=target, send_sem=send, recv_sem=recv,
            device_id=there, device_id_type=MESH,
        )

    first = copy(src.at[pl.ds((1 - core) * 16, 16)], core_buf, core_send, core_recv, core_peer)
    first.start()
    first.wait()

    @pl.loop(0, 16)
    def _(s):
        held[s] = (src[core * 16 + s].astype(F32) + core_buf[s].astype(F32)).astype(BF16)

    second = copy(held.at[pl.ds((1 - x) * 8, 8)], x_buf, x_send, x_recv, x_peer)
    second.start()
    second.wait()

    @pl.loop(0, 8)
    def _(s):
        x_buf[s] = (held[x * 8 + s].astype(F32) + x_buf[s].astype(F32)).astype(BF16)

    third = [
        copy(x_buf.at[(z + d) % Z], z_buf.at[d - 1], z_send.at[d - 1], z_recv.at[d - 1], z_peers[d - 1])
        for d in range(1, Z)
    ]
    for c in third:
        c.start()
    for c in third:
        c.wait()
    total = x_buf[z].astype(F32)
    for d in range(Z - 1):
        total = total + z_buf[d].astype(F32)
    mine = core * 16 + x * 8 + z
    weights[...] = total[BIAS_ROWS:].astype(BF16)
    lat_buf[lat] = total[BIAS_ROWS:].astype(BF16)
    fourth = [
        copy(weights, lat_buf.at[lat], lat_send.at[d - 1], lat_recv.at[d - 1], lat_peers[d - 1])
        for d in range(1, LATS)
    ]
    for c in fourth:
        c.start()
    out[mine, :BIAS_ROWS, :] = total[:BIAS_ROWS].astype(BF16)
    part = out.at[mine, pl.ds(0, BIAS_ROWS)]
    gather = [
        copy(part, part, gz_send.at[d - 1], gz_recv.at[d - 1], z_peers[d - 1]) for d in range(1, Z)
    ]
    for c in gather:
        c.start()
    for c in fourth:
        c.wait()
    total = lat_buf[0].astype(F32)
    for i in range(1, LATS):
        total = total + lat_buf[i].astype(F32)
    out[mine, BIAS_ROWS:, :] = total.astype(BF16)
    part = out.at[mine, pl.ds(BIAS_ROWS, WEIGHT_ROWS)]
    gather_weights = [
        copy(part, part, gw_send.at[d - 1], gw_recv.at[d - 1], z_peers[d - 1]) for d in range(1, Z)
    ]
    for c in gather_weights:
        c.start()
    for c in gather + gather_weights:
        c.wait()
    part = out.at[pl.ds(core * 16 + x * 8, 8)]
    c = copy(part, part, gx_send, gx_recv, x_peer)
    c.start()
    c.wait()
    part = out.at[pl.ds(core * 16, 16)]
    c = copy(part, part, gc_send, gc_recv, core_peer)
    c.start()
    c.wait()


def sums(packed):
    dma = pltpu.SemaphoreType.DMA
    return pl.pallas_call(
        sums_kernel,
        out_shape=jax.ShapeDtypeStruct((LONS, SHARD, 128), BF16),
        in_specs=[vmem_spec()],
        out_specs=vmem_spec(),
        scratch_shapes=[
            pltpu.VMEM((16, SHARD, 128), BF16),
            pltpu.VMEM((8, SHARD, 128), BF16),
            pltpu.VMEM((Z - 1, SHARD, 128), BF16),
            pltpu.VMEM((LATS, WEIGHT_ROWS, 128), BF16),
            pltpu.VMEM((16, SHARD, 128), BF16),
            pltpu.VMEM((WEIGHT_ROWS, 128), BF16),
            dma, dma, dma, dma,
            dma((Z - 1,)), dma((Z - 1,)), dma((LATS - 1,)), dma((LATS - 1,)),
            dma((Z - 1,)), dma((Z - 1,)), dma((Z - 1,)), dma((Z - 1,)),
            dma, dma, dma, dma,
        ],
        compiler_params=params(collective_id=2, has_side_effects=True),
        name="sums",
    )(packed)


def unpack_kernel(src, bias_ref, qkv_ref, out_ref, gain_ref, flat, weight):
    for s in range(LONS):
        flat[s * BIAS_ROWS : (s + 1) * BIAS_ROWS, :] = src[s, :BIAS_ROWS, :].astype(F32)
    for s in range(16):
        weight[s * 48 : (s + 1) * 48, :128] = src[s, BIAS_ROWS:, :].astype(F32)
    for s in range(8):
        pair = src[16 + s, BIAS_ROWS:, :].astype(F32)
        weight[s * 48 : (s + 1) * 48, 128:] = pair[:, :64]
        weight[384 + s * 48 : 384 + (s + 1) * 48, 128:] = pair[:, 64:]
    gain = src[24, BIAS_ROWS : BIAS_ROWS + 16, :].astype(F32)
    gain_ref[:, :128] = gain[0:1, :]
    gain_ref[:, 128:] = gain[1:2, :64]
    qkv_ref[...] = jnp.transpose(weight[: 3 * WIDTH, :])
    out_ref[...] = weight[3 * WIDTH :, :]
    column = lax.broadcasted_iota(jnp.int32, (HALF, TOKENS), 1)
    for g in range(2):
        for w in range(2):
            rows = (TOKENS, HALF)[w]
            at = g * 1512 + w * 1008
            tail = flat[at + HEADS * rows : at + (HEADS + 1) * rows, :]
            for h in range(HEADS):
                main = flat[at + h * rows : at + (h + 1) * rows, :]
                value = jnp.concatenate([main, tail[:, 16 * h : 16 * h + 16]], axis=1)
                if w == 0:
                    bias_ref[g, w, h] = value
                else:
                    bias_ref[g, w, h, :HALF, :] = jnp.where(column < HALF, value, 0.0)
                    bias_ref[g, w, h, HALF:, :] = jnp.where(column < HALF, 0.0, value)


def unpack(src):
    return pl.pallas_call(
        unpack_kernel,
        out_shape=(
            jax.ShapeDtypeStruct((2, 2, HEADS, TOKENS, TOKENS), F32),
            jax.ShapeDtypeStruct((WIDTH, 3 * WIDTH), F32),
            jax.ShapeDtypeStruct((WIDTH, WIDTH), F32),
            jax.ShapeDtypeStruct((1, WIDTH), F32),
        ),
        in_specs=[vmem_spec()],
        out_specs=(vmem_spec(),) * 4,
        scratch_shapes=[pltpu.VMEM((BIAS_ALL, 128), F32), pltpu.VMEM((4 * WIDTH, WIDTH), F32)],
        compiler_params=params(),
        name="unpack",
    )(src)


def local(fields, out_grad, gain, qkv_weight, out_weight, window_bias):
    tables = window_bias.reshape(2, 2, HEADS, TOKENS, TOKENS)
    a, b = pack_in(fields, out_grad)
    a, b, c = halo(1, a, b)
    xw, gw = assemble(fields, out_grad, a, b, c)
    ig, packed = compute(xw, gw, gain, qkv_weight, out_weight, tables)
    tiles, e, d = pack_out(ig)
    e, d, f = halo(-1, e, d)
    input_grad = place(tiles, e, d, f)
    bias, qkv_grad, out_weight_grad, gain_grad = unpack(sums(packed))
    return (
        input_grad,
        qkv_grad,
        out_weight_grad,
        gain_grad.reshape(WIDTH),
        bias.reshape(2, 2, HEADS, TOKENS * TOKENS),
    )


def solution(mesh):
    in_specs = (
        P(None, "lat", "lon", None),
        P(None, "lat", "lon", None),
        P(),
        P(),
        P(),
        P("lat", None, None, None),
    )
    out_specs = (P(None, "lat", "lon", None), P(), P(), P(), P("lat", None, None, None))
    return jax.shard_map(local, mesh=mesh, in_specs=in_specs, out_specs=out_specs, check_vma=False)
```

time: 734 us -> 164 us (0.22)
  waiting for transfers between devices: 375 us -> 0 us
  Pallas kernels: 0 us -> 142 us
  local copies, waits for them, and re-layouts: 140 us -> 20.8 us
  blocking collectives: 83.7 us -> 0 us
  matrix products: 59 us -> 0 us
  other arithmetic: 40.6 us -> 0 us
  starting transfers between devices: 16.6 us -> 0 us
  between operations: 14.4 us -> 0.68 us
    psum x2 -> x0, waiting for transfers between devices: 368 us -> none  [the longest x1 229 us: local(): bias_total = lax.psum(bias_flat, 'lon')]
    pallas_call x0 -> x9, Pallas kernels: none -> 142 us  [the longest x1 60.8 us: sums(): pl.pallas_call(sums_kernel, out_shape=jax.ShapeDtypeStruct((LONS, SHARD,...]
    psum x1 -> x0, blocking collectives: 83.7 us -> none  [local(): lax.psum((qkv_sum, out_sum, gain_part), ('lat', 'lon'))]
    reshape x42 -> x4, local copies, waits for them, and re-layouts: 60.3 us -> 12.7 us  [the longest x2 6.46 us: local(): tables = window_bias.reshape(2, 2, HEADS, TOKENS, TOKENS)]
    dot_general x30 -> x0, matrix products: 47.4 us -> none  [the longest x3 6.15 us: window_row(): out_part = jnp.dot(attended.T, upstream, preferred_element_type=f32)]
    dynamic_slice x9 -> x0, local copies, waits for them, and re-layouts: 16.8 us -> none  [local(): lax.scan(visit, start, (stack_rows(shifted_in), stack_rows(shifted_grad),...]
    ppermute x6 -> x0, starting transfers between devices: 16.5 us -> none  [the longest x3 9.34 us: from_behind(): return lax.ppermute(block, axis, route)]
    reduce_sum x9 -> x0, other arithmetic: 16.3 us -> none  [the longest x3 9.95 us: window_row(): bias_part = jnp.sum(grad_scores, axis=1)]
  transfers between devices with their start and end apart: 8 -> 0, of which waited for: 4 -> 0; matrix products, arithmetic and copies ran while one was open for 5% -> 0% of each run, Pallas kernels for 0% -> 0%
where the time goes in v1:
time: 164 us; the launch traced here: 163 us
  Pallas kernels  142 us (87%)
  local copies, waits for them, and re-layouts  20.8 us (13%)
    pallas_call x1, Pallas kernels, sums(): pl.pallas_call(sums_kernel, out_shape=jax.ShapeDtypeStruct((LONS, SHARD,...  60.8 us
    pallas_call x1, Pallas kernels, compute(): pl.pallas_call(compute_kernel, grid=(2, 3), out_shape=(jax.ShapeDtypeStru...  35.1 us
    pallas_call x2, Pallas kernels, halo(): pl.pallas_call(lambda *refs: halo_kernel(step, *refs), out_shape=(jax.Sha...  30.6 us
    unnamed x4, local copies, waits for them, and re-layouts  8.12 us
    reshape x2, local copies, waits for them, and re-layouts, local(): tables = window_bias.reshape(2, 2, HEADS, TOKENS, TOKENS)  6.46 us
    reshape x2, local copies, waits for them, and re-layouts, local(): bias.reshape(2, 2, HEADS, TOKENS * TOKENS)  6.23 us
    pallas_call x1, Pallas kernels, unpack(): pl.pallas_call(unpack_kernel, out_shape=(jax.ShapeDtypeStruct((2, 2, HEAD...  3.77 us
    pallas_call x1, Pallas kernels, assemble(): pl.pallas_call(assemble_kernel, out_shape=(shape, shape), in_specs=[vmem_...  3.48 us

profile of v1, /device:TPU:1, one launch (start us, length us, event | category | flops | bytes accessed | tf_op | source)
XLA Modules:
  0.0 163.4 jit_solution(10394699482875490134)
XLA Ops:
  0.6 2.1 %copy.21.fields_ref = bf16[4,24,12,192]{3,2,1,0:T(8,128)(2,1)} copy(bf16[4,24,12,192]{3,1,2,0:T(8,128)(2,1)} %param.6) | data formatting | bytes 884736 | tf_op args[0]
  2.7 2.1 %copy.22.grad_ref = bf16[4,24,12,192]{3,2,1,0:T(8,128)(2,1)} copy(bf16[4,24,12,192]{3,1,2,0:T(8,128)(2,1)} %param.7) | data formatting | bytes 884736 | tf_op args[1]
  4.8 2.3 %pack_in.1 = (bf16[2,288,192]{2,1,0:T(8,128)(2,1)}, bf16[2,288,192]{2,1,0:T(8,128)(2,1)}) custom-call(bf16[4,24,12,192]{3,2,1,0:T(8,128)(2,1)} %copy.21.fields_ref, bf16[4,24,12,192]{3,2,1,0:T(8,128)(2,1)} %copy.22.grad_ref), custom_call_target="tpu_custom_call" | custom-call | tf_op jit(solution)/shard_map/pack_in/pallas_call | solution.py:60
  7.1 19.4 %halo.2 = (bf16[2,288,192]{2,1,0:T(8,128)(2,1)}, bf16[2,288,192]{2,1,0:T(8,128)(2,1)}, bf16[2,80,192]{2,1,0:T(8,128)(2,1)}) custom-call(bf16[2,288,192]{2,1,0:T(8,128)(2,1)} %get-tuple-element.24.refs_0_, bf16[2,288,192]{2,1,0:T(8,128)(2,1)} %get-tuple-element.25.refs_1_), custom_call_target="tpu_custom_call" | custom-call | tf_op jit(solution)/shard_map/halo/pallas_call | solution.py:105
  26.6 3.5 %assemble.1 = (bf16[2,3,2,144,192]{4,3,2,1,0:T(8,128)(2,1)}, bf16[2,3,2,144,192]{4,3,2,1,0:T(8,128)(2,1)}) custom-call(bf16[4,24,12,192]{3,2,1,0:T(8,128)(2,1)} %copy.21.fields_ref, bf16[4,24,12,192]{3,2,1,0:T(8,128)(2,1)} %copy.22.grad_ref, bf16[2,288,192]{2,1,0:T(8,128)(2,1)} %get-tuple-element.26.a_ref, bf16[2,288,192]{2,1,0:T(8,128)(2,1)} %get-tuple-element.27.b_ref, ...), custom_call_target="tpu_custom_call" | custom-call | tf_op jit(solution)/shard_map/assemble/pallas_call | solution.py:155
  30.0 4.3 %reshape.23 = f32[2,2,6,144,144]{4,3,1,2,0:T(8,128)S(1)} reshape(f32[2,2,6,20736]{3,1,2,0:T(2,128)} %param.11) | data formatting | bytes 3981312 | tf_op jit(solution)/shard_map/reshape | solution.py:585
  34.4 2.1 %copy.24.bias_ref = f32[2,2,6,144,144]{4,3,2,1,0:T(8,128)} copy(f32[2,2,6,144,144]{4,3,1,2,0:T(8,128)S(1)} %reshape.23) | data formatting | bytes 3981312 | tf_op jit(solution)/shard_map/reshape | solution.py:585
  36.5 1.8 %copy.23 = bf16[192,576]{0,1:T(8,128)(2,1)} copy(bf16[192,576]{1,0:T(8,128)(2,1)} %qkv_ref.1) | data formatting | bytes 442368 | tf_op args[3]
  38.3 35.1 %windows.1 = (bf16[2,3,2,144,192]{4,3,2,1,0:T(8,128)(2,1)}, bf16[32,144,128]{2,1,0:T(8,128)(2,1)}) custom-call(bf16[2,3,2,144,192]{4,3,2,1,0:T(8,128)(2,1)} %get-tuple-element.29.x_ref, bf16[2,3,2,144,192]{4,3,2,1,0:T(8,128)(2,1)} %get-tuple-element.30.g_ref, f32[1,192]{1,0:T(1,128)} %bitcast.8, bf16[192,576]{1,0:T(8,128)(2,1)} %qkv_ref.1, ...), custom_call_target="tpu_custom_call" | custom-call | tf_op jit(solution)/shard_map/windows/pallas_call | solution.py:317
  73.4 60.8 %sums.1.src = bf16[32,144,128]{2,1,0:T(8,128)(2,1)} custom-call(bf16[32,144,128]{2,1,0:T(8,128)(2,1)} %get-tuple-element.38.src), custom_call_target="tpu_custom_call" | custom-call | tf_op jit(solution)/shard_map/sums/pallas_call | solution.py:515
  134.2 3.8 %unpack.1 = (f32[2,2,6,144,144]{4,3,2,1,0:T(8,128)}, f32[192,576]{1,0:T(8,128)}, f32[192,192]{1,0:T(8,128)}, f32[1,192]{1,0:T(1,128)}) custom-call(bf16[32,144,128]{2,1,0:T(8,128)(2,1)} %sums.1.src), custom_call_target="tpu_custom_call" | custom-call | tf_op jit(solution)/shard_map/unpack/pallas_call | solution.py:568
  138.0 3.9 %reshape.26 = f32[2,2,6,20736]{3,2,1,0:T(8,128)S(1)} reshape(f32[2,2,6,144,144]{4,3,2,1,0:T(8,128)} %get-tuple-element.42) | data formatting | bytes 3981312 | tf_op jit(solution)/shard_map/reshape | solution.py:599
  141.9 2.3 %copy.27 = f32[2,2,6,20736]{3,1,2,0:T(2,128)} copy(f32[2,2,6,20736]{3,2,1,0:T(8,128)S(1)} %reshape.26) | data formatting | bytes 3981312 | tf_op jit(solution)/shard_map/reshape | solution.py:599
  144.2 3.2 %pack_out.1 = (f32[4,30,12,192]{3,2,1,0:T(8,128)}, bf16[1,288,192]{2,1,0:T(8,128)(2,1)}, bf16[1,368,192]{2,1,0:T(8,128)(2,1)}) custom-call(bf16[2,3,2,144,192]{4,3,2,1,0:T(8,128)(2,1)} %get-tuple-element.31.ig_ref), custom_call_target="tpu_custom_call" | custom-call | tf_op jit(solution)/shard_map/pack_out/pallas_call | solution.py:371
  147.4 11.2 %halo.3 = (bf16[1,288,192]{2,1,0:T(8,128)(2,1)}, bf16[1,368,192]{2,1,0:T(8,128)(2,1)}, bf16[1,80,192]{2,1,0:T(8,128)(2,1)}) custom-call(bf16[1,288,192]{2,1,0:T(8,128)(2,1)} %get-tuple-element.33.refs_0_, bf16[1,368,192]{2,1,0:T(8,128)(2,1)} %get-tuple-element.34.refs_1_), custom_call_target="tpu_custom_call" | custom-call | tf_op jit(solution)/shard_map/halo/pallas_call | solution.py:105
  158.6 2.7 %place.1 = bf16[4,24,12,192]{3,2,1,0:T(8,128)(2,1)} custom-call(f32[4,30,12,192]{3,2,1,0:T(8,128)} %get-tuple-element.32.tile_ref, bf16[1,288,192]{2,1,0:T(8,128)(2,1)} %get-tuple-element.35.e_ref, bf16[1,368,192]{2,1,0:T(8,128)(2,1)} %get-tuple-element.36.d_ref, bf16[1,80,192]{2,1,0:T(8,128)(2,1)} %get-tuple-element.37.f_ref), custom_call_target="tpu_custom_call" | custom-call | tf_op jit(solution)/shard_map/place/pallas_call | solution.py:408
  161.3 2.1 %copy.26 = bf16[4,24,12,192]{3,1,2,0:T(8,128)(2,1)} copy(bf16[4,24,12,192]{3,2,1,0:T(8,128)(2,1)} %place.1) | data formatting | bytes 884736

commit v2 on v0

v2 whole, which is shorter than its diff:
```python
import jax
import jax.numpy as jnp
from jax import lax
from jax.experimental import pallas as pl
from jax.experimental.pallas import tpu as pltpu
from jax.sharding import PartitionSpec as P

F32 = jnp.float32
BF16 = jnp.bfloat16
MESH = pl.DeviceIdType.MESH

EPS = 1e-05
MASKED = -1e30
LOG2E = 1.4426950408889634

LEVELS = 4
ROWS = 24
COLS = 12
WIDTH = 192
HEADS = 6
HEAD = 32
TOKENS = 144
HALF = 72
LATS = 8
LONS = 32
Z = 8

CHUNK_ROWS = (32, 16, 32, 16, 48)
BIAS_CHUNKS = ((1, 0), (1, 1), (0, 0), (0, 1))
WEIGHTS = 4

VMEM_LIMIT = 56 * 1024 * 1024


def dot(a, b, contract=(1, 0)):
    return lax.dot_general(
        a, b, (((contract[0],), (contract[1],)), ((), ())), preferred_element_type=F32
    )


def remote(source, target, send, recv, there):
    return pltpu.make_async_remote_copy(
        src_ref=source, dst_ref=target, send_sem=send, recv_sem=recv, device_id=there, device_id_type=MESH
    )


def put_cells(own, tiles_of, win, g, k, lat):
    @pl.loop(0, LEVELS)
    def _(z):
        lev = (z + 1) % LEVELS
        w, zl = z // 2, z % 2
        for lp in range(12):
            row = 12 * g + lp - 6
            at = lp * 6
            if row >= ROWS:
                win[k, w, g, 0, zl, at : at + 6, :] = jnp.zeros((6, WIDTH), F32)
                win[k, w, g, 1, zl, at : at + 6, :] = jnp.zeros((6, WIDTH), F32)
                continue
            if row < 0:
                tile = tiles_of[lev, (row + 6) * 12 : (row + 6) * 12 + 12, k * WIDTH : (k + 1) * WIDTH].astype(F32)
                tile = jnp.where(lat == 0, 0.0, tile)
            else:
                tile = own[lev, row].astype(F32)
            win[k, w, g, 0, zl, at : at + 6, :] = tile[3:9]
            win[k, w, g, 1, zl, at : at + 3, :] = tile[9:12]


def put_east(east, corner, win, g, k, lat):
    @pl.loop(0, LEVELS)
    def _(z):
        lev = (z + 1) % LEVELS
        w, zl = z // 2, z % 2
        lanes = slice(k * WIDTH, (k + 1) * WIDTH)
        for lp in range(12):
            row = 12 * g + lp - 6
            if row >= ROWS:
                continue
            if row < 0:
                cells = corner[lev, (row + 6) * 3 : (row + 6) * 3 + 3, lanes]
                cells = jnp.where(lat == 0, 0.0, cells)
            else:
                at = ((row - 18) % ROWS) * 3
                cells = east[lev, at : at + 3, lanes]
            win[k, w, g, 1, zl, lp * 6 + 3 : lp * 6 + 6, :] = cells


def window(win, w, g, n, gain, qkv_ref, qkv_t_ref, out_ref, masked, bias_acc, weight_acc, gain_acc):
    scale = HEAD ** (-0.5)
    x = win[0, w, g, n].reshape(TOKENS, WIDTH)
    centred = x - jnp.mean(x, axis=-1, keepdims=True)
    inv_std = lax.rsqrt(jnp.mean(centred * centred, axis=-1, keepdims=True) + EPS)
    standard = centred * inv_std
    normed = (standard * gain).astype(BF16)
    upstream32 = win[1, w, g, n].reshape(TOKENS, WIDTH)
    upstream = upstream32.astype(BF16)
    projected = dot(normed, qkv_ref[...]).astype(BF16)
    queries_t = dot(qkv_t_ref[:WIDTH, :], normed, (1, 1)).astype(BF16)
    attended_grad = dot(upstream, out_ref[...], (1, 1)).astype(BF16)
    attended_grad_t = dot(out_ref[...], upstream, (1, 1)).astype(BF16)
    lane = lax.broadcasted_iota(jnp.int32, (TOKENS, WIDTH), 1)
    own = [(lane // HEAD) == h for h in range(HEADS)]
    zero = jnp.zeros((), BF16)
    queries_all = jnp.concatenate([jnp.where(own[h], projected[:, :WIDTH], zero) for h in range(HEADS)], axis=0)
    upper_all = jnp.concatenate([jnp.where(own[h], attended_grad, zero) for h in range(HEADS)], axis=0)
    keys = projected[:, WIDTH : 2 * WIDTH]
    values = projected[:, 2 * WIDTH :]
    scores_all = dot(queries_all, keys, (1, 1))
    grads_all = dot(upper_all, values, (1, 1))
    keys_parts, values_parts, lows, scores_lows = [], [], [], []
    for h in range(HEADS):
        at = slice(h * TOKENS, (h + 1) * TOKENS)
        rows = slice(h * HEAD, (h + 1) * HEAD)
        scores = scores_all[at] * (scale * LOG2E) + masked[h]
        exps = jnp.exp2(scores - jnp.max(scores, axis=-1, keepdims=True))
        attention = exps * (1.0 / jnp.sum(exps, axis=-1, keepdims=True))
        low = attention.astype(BF16)
        attention_grad = grads_all[at]
        delta = jnp.sum(attention * attention_grad, axis=-1, keepdims=True)
        scores_grad = attention * (attention_grad - delta)
        bias_acc[h] += scores_grad
        scores_low = scores_grad.astype(BF16)
        lows.append(low)
        scores_lows.append(scores_low)
        values_parts.append(dot(attended_grad_t[rows], low).astype(BF16))
        keys_parts.append((dot(queries_t[rows], scores_low) * scale).astype(BF16))
    attended_all = dot(jnp.concatenate(lows, axis=0), values)
    queries_grad_all = dot(jnp.concatenate(scores_lows, axis=0), keys)
    attended_sum = jnp.zeros((TOKENS, WIDTH), F32)
    queries_sum = jnp.zeros((TOKENS, WIDTH), F32)
    for h in range(HEADS):
        at = slice(h * TOKENS, (h + 1) * TOKENS)
        attended_sum = jnp.where(own[h], attended_all[at], attended_sum)
        queries_sum = jnp.where(own[h], queries_grad_all[at], queries_sum)
    attended_t = jnp.transpose(attended_sum).astype(BF16)
    queries_grad_t = (jnp.transpose(queries_sum) * scale).astype(BF16)
    projected_grad_t = jnp.concatenate([queries_grad_t] + keys_parts + values_parts, axis=0)
    weight_acc[3 * WIDTH :, :] += dot(attended_t, upstream)
    weight_acc[: 3 * WIDTH, :] += dot(projected_grad_t, normed)
    shifted_t = dot(qkv_ref[...], projected_grad_t)
    grad = jnp.transpose(shifted_t).astype(BF16).astype(F32)
    product = grad * standard
    gain_acc[...] += jnp.sum(product, axis=0, keepdims=True)
    scaled = grad * gain
    ig = upstream32 + inv_std * (
        scaled
        - jnp.mean(scaled, axis=-1, keepdims=True)
        - standard * jnp.mean(product * gain, axis=-1, keepdims=True)
    )
    win[0, w, g, n] = ig.reshape(2, HALF, WIDTH)


def mask_bias(masked, bias_ref, w, g, lat):
    q = lax.broadcasted_iota(jnp.int32, (TOKENS, 1), 0)
    k = lax.broadcasted_iota(jnp.int32, (1, TOKENS), 1)
    half = ((q >= HALF) != (k >= HALF)) & (w == 1)
    q_low = ((q // 6) % 12) < 6
    k_low = ((k // 6) % 12) < 6
    top = (q_low | k_low) & (g == 0) & (lat == 0)
    bottom = jnp.logical_not(q_low & k_low) & (g == 2)
    blocked = half | top | bottom
    table = jnp.minimum(g, 1)
    for h in range(HEADS):
        masked[h] = jnp.where(blocked, MASKED, bias_ref[table, w, h] * LOG2E)


def fold(w, take, flat, src):
    rows = (TOKENS, HALF)[w]
    tails = []
    for h in range(HEADS):
        value = take(h)
        flat[h * rows : (h + 1) * rows, :] = value[:, :128]
        tails.append(value[:, 128:])
    tails.append(jnp.zeros((rows, 32), F32))
    flat[HEADS * rows : 7 * rows, :] = jnp.concatenate(tails, axis=1)
    flat[7 * rows : 7 * rows + (16, 8)[w], :] = jnp.zeros(((16, 8)[w], 128), F32)
    each = (32, 16)[w]
    src[...] = flat[: LONS * each, :].astype(BF16).reshape(LONS, each, 128)


def fold_weights(weight_acc, gain_acc, src):
    for s in range(16):
        src[s] = weight_acc[s * 48 : (s + 1) * 48, :128].astype(BF16)
    for s in range(8):
        pair = jnp.concatenate(
            [weight_acc[s * 48 : (s + 1) * 48, 128:], weight_acc[384 + s * 48 : 384 + (s + 1) * 48, 128:]], axis=1
        )
        src[16 + s] = pair.astype(BF16)
    total = gain_acc[...]
    left = jnp.broadcast_to(total[:, :128], (48, 128))
    right = jnp.concatenate([total[:, 128:], jnp.zeros((1, 64), F32)], axis=1)
    right = jnp.broadcast_to(right, (48, 128))
    row = lax.broadcasted_iota(jnp.int32, (48, 128), 0)
    src[24] = jnp.where(row == 0, left, jnp.where(row == 1, right, 0.0)).astype(BF16)
    src[25:] = jnp.zeros((LONS - 25, 48, 128), BF16)


def unfold(w, out, flat, bias_out):
    rows, each = (TOKENS, HALF)[w], (32, 16)[w]
    flat[: LONS * each, :] = out[...].reshape(LONS * each, 128).astype(F32)
    tail = flat[HEADS * rows : 7 * rows, :]
    column = lax.broadcasted_iota(jnp.int32, (HALF, TOKENS), 1)
    for h in range(HEADS):
        value = jnp.concatenate([flat[h * rows : (h + 1) * rows, :], tail[:, 16 * h : 16 * h + 16]], axis=1)
        if w == 0:
            bias_out[h] = value
        else:
            bias_out[h, :HALF, :] = jnp.where(column < HALF, value, 0.0)
            bias_out[h, HALF:, :] = jnp.where(column < HALF, 0.0, value)


def unfold_weights(out, weight, qkv_ref, out_ref, gain_ref):
    for s in range(16):
        weight[s * 48 : (s + 1) * 48, :128] = out[s].astype(F32)
    for s in range(8):
        pair = out[16 + s].astype(F32)
        weight[s * 48 : (s + 1) * 48, 128:] = pair[:, :64]
        weight[384 + s * 48 : 384 + (s + 1) * 48, 128:] = pair[:, 64:]
    gain = out[24, 0:16, :].astype(F32)
    gain_ref[:, :128] = gain[0:1, :]
    gain_ref[:, 128:] = gain[1:2, :64]
    qkv_ref[...] = jnp.transpose(weight[: 3 * WIDTH, :])
    out_ref[...] = weight[3 * WIDTH :, :]


def kernel(
    fields_hbm, grad_hbm, gain_ref, qkv_ref, qkv_t_ref, out_w_ref, bias_hbm,
    input_grad_hbm, qkv_grad_ref, out_grad_ref, gain_grad_ref, bias_grad_hbm,
    fields, grads, bias, bias_out, cells_out,
    a_send, b_send, a_recv, b_recv, c_recv, pack32, east32, corner32,
    win, masked, bias_acc, weight_acc, gain_acc, flat,
    tiles, e_send, d_send, e_recv, d_recv, f_recv,
    src0, src1, src2, src3, src4, core0, core1, core2, core3, core4,
    xb0, xb1, xb2, xb3, xb4, zb0, zb1, zb2, zb3, zb4, out0, out1, out2, out3, out4,
    lat_send_buf, lat_buf,
    local_sem, halo_send, halo_recv, pair_send, pair_recv, z_send, z_recv, gz_send, gz_recv, lat_send, lat_recv,
):
    lat = lax.axis_index("lat")
    lon = lax.axis_index("lon")
    last = lat == LATS - 1
    z, x, core = lon // 4, (lon // 2) % 2, lon % 2
    up, down = (lat + LATS - 1) % LATS, (lat + 1) % LATS
    west, east = (lon + LONS - 1) % LONS, (lon + 1) % LONS

    def at_lon(zz, xx, cc):
        return (lat, zz * 4 + xx * 2 + cc)

    core_peer = at_lon(z, x, 1 - core)
    x_peer = at_lon(z, 1 - x, core)
    z_peers = [at_lon((z + d) % Z, x, core) for d in range(1, Z)]
    lat_peers = [((lat + d) % LATS, lon) for d in range(1, LATS)]

    loads = [
        pltpu.make_async_copy(fields_hbm, fields, local_sem.at[0]),
        pltpu.make_async_copy(grad_hbm, grads, local_sem.at[1]),
        pltpu.make_async_copy(bias_hbm, bias, local_sem.at[2]),
    ]
    for c in loads:
        c.start()
    barrier = pltpu.get_barrier_semaphore()
    greeted = [core_peer, x_peer, (lat, west), (lat, east), (down, west), (up, east)] + z_peers + lat_peers
    for there in greeted:
        pl.semaphore_signal(barrier, inc=1, device_id=there, device_id_type=MESH)

    loads[0].wait()
    loads[1].wait()

    @pl.loop(0, LEVELS)
    def _(lev):
        for k, own in enumerate((fields, grads)):
            for r in range(ROWS):
                at = ((r - 18) % ROWS) * 3
                pack32[lev, at : at + 3, k * WIDTH : (k + 1) * WIDTH] = own[lev, r].astype(F32)[0:3]
        b_send[lev] = pack32[lev, 0:80].astype(BF16)
        for k, own in enumerate((fields, grads)):
            for r in range(6):
                pack32[lev, r * 12 : r * 12 + 12, k * WIDTH : (k + 1) * WIDTH] = own[lev, 18 + r].astype(F32)
        a_send[lev] = pack32[lev, 0:80].astype(BF16)

    pl.semaphore_wait(barrier, len(greeted))
    b_copy = remote(b_send, b_recv, halo_send.at[0], halo_recv.at[0], (lat, west))
    a_copy = remote(a_send, a_recv, halo_send.at[1], halo_recv.at[1], (down, lon))
    c_copy = remote(b_send.at[:, 0:32], c_recv, halo_send.at[2], halo_recv.at[2], (down, west))
    b_copy.start()

    @pl.when(lat < LATS - 1)
    def _():
        a_copy.start()
        c_copy.start()

    weight_acc[...] = jnp.zeros_like(weight_acc)
    gain_acc[...] = jnp.zeros_like(gain_acc)
    for k, own in enumerate((fields, grads)):
        for g in (1, 2):
            put_cells(own, a_recv, win, g, k, lat)
    loads[2].wait()
    b_copy.wait()
    east32[...] = b_recv[...].astype(F32)
    for k in range(2):
        for g in (1, 2):
            put_east(east32, corner32, win, g, k, lat)

    srcs = (src0, src1, src2, src3, src4)
    core_bufs = (core0, core1, core2, core3, core4)
    x_bufs = (xb0, xb1, xb2, xb3, xb4)
    z_bufs = (zb0, zb1, zb2, zb3, zb4)
    outs = (out0, out1, out2, out3, out4)
    mine = core * 16 + x * 8 + z

    def core_copy(c):
        return remote(
            srcs[c].at[pl.ds((1 - core) * 16, 16)], core_bufs[c], pair_send.at[c, 0], pair_recv.at[c, 0], core_peer
        )

    def x_copy(c):
        return remote(
            srcs[c].at[pl.ds(core * 16 + (1 - x) * 8, 8)], x_bufs[c], pair_send.at[c, 1], pair_recv.at[c, 1], x_peer
        )

    def z_copies(c):
        return [
            remote(
                srcs[c].at[core * 16 + x * 8 + (z + d) % Z], z_bufs[c].at[d - 1],
                z_send.at[c, d - 1], z_recv.at[c, d - 1], z_peers[d - 1],
            )
            for d in range(1, Z)
        ]

    def gz_copies(c):
        part = outs[c].at[mine]
        return [remote(part, part, gz_send.at[c, d - 1], gz_recv.at[c, d - 1], z_peers[d - 1]) for d in range(1, Z)]

    def gx_copy(c):
        part = outs[c].at[pl.ds(core * 16 + x * 8, 8)]
        return remote(part, part, pair_send.at[c, 2], pair_recv.at[c, 2], x_peer)

    def gc_copy(c):
        part = outs[c].at[pl.ds(core * 16, 16)]
        return remote(part, part, pair_send.at[c, 3], pair_recv.at[c, 3], core_peer)

    lat_copies = [
        remote(lat_send_buf, lat_buf.at[lat], lat_send.at[d - 1], lat_recv.at[d - 1], lat_peers[d - 1])
        for d in range(1, LATS)
    ]

    def start(copies):
        for c in copies:
            c.start()

    def wait(copies):
        for c in copies:
            c.wait()

    def add_core(c):
        core_copy(c).wait()
        half = pl.ds(core * 16, 16)
        srcs[c][half] = (srcs[c][half].astype(F32) + core_bufs[c][...].astype(F32)).astype(BF16)
        x_copy(c).start()

    def add_x(c):
        x_copy(c).wait()
        part = pl.ds(core * 16 + x * 8, 8)
        srcs[c][part] = (srcs[c][part].astype(F32) + x_bufs[c][...].astype(F32)).astype(BF16)
        start(z_copies(c))

    def add_z(c):
        wait(z_copies(c))
        total = srcs[c][mine].astype(F32)
        for d in range(Z - 1):
            total = total + z_bufs[c][d].astype(F32)
        return total.astype(BF16)

    def gather_z(c):
        outs[c][mine] = add_z(c)
        start(gz_copies(c))

    def gather_x(c):
        wait(gz_copies(c))
        gx_copy(c).start()

    def gather_core(c):
        gx_copy(c).wait()
        gc_copy(c).start()

    def bias_store(c):
        g, w = BIAS_CHUNKS[c]
        return pltpu.make_async_copy(bias_out.at[g, w], bias_grad_hbm.at[g, w], local_sem.at[3 + c])

    def finish(c):
        gc_copy(c).wait()
        g, w = BIAS_CHUNKS[c]
        unfold(w, outs[c], flat, bias_out.at[g, w])
        bias_store(c).start()

    @pl.loop(0, 6)
    def _(t):
        early = jnp.where(t < 4, 1, 0)
        g = early * (2 - t % 2)
        w = early * (t // 2) + (1 - early) * (t - 4)

        @pl.when(t == 4)
        def _():
            @pl.when(lat < LATS - 1)
            def _():
                a_copy.wait_send()
                c_copy.wait_send()

            @pl.when(lat > 0)
            def _():
                a_copy.wait_recv()
                c_copy.wait_recv()

            corner32[...] = c_recv[...].astype(F32)
            for k, own in enumerate((fields, grads)):
                put_cells(own, a_recv, win, 0, k, lat)
                put_east(east32, corner32, win, 0, k, lat)

        @pl.when((t == 0) | (t == 2) | (t >= 4))
        def _():
            bias_acc[...] = jnp.zeros_like(bias_acc)

        @pl.when((g < 2) | last)
        def _():
            mask_bias(masked, bias, w, g, lat)
            gain = gain_ref[...]
            for n in range(2):
                window(win, w, g, n, gain, qkv_ref, qkv_t_ref, out_w_ref, masked, bias_acc, weight_acc, gain_acc)

        @pl.when(t == 1)
        def _():
            fold(0, lambda h: bias_acc[h], flat, src0)
            core_copy(0).start()

        @pl.when(t == 3)
        def _():
            fold(1, lambda h: bias_acc[h, :HALF, :] + bias_acc[h, HALF:, :], flat, src1)
            core_copy(1).start()
            add_core(0)

        @pl.when(t == 4)
        def _():
            fold(0, lambda h: bias_acc[h], flat, src2)
            core_copy(2).start()
            add_core(1)
            add_x(0)

        @pl.when(t == 5)
        def _():
            fold_weights(weight_acc, gain_acc, src4)
            core_copy(4).start()
            fold(1, lambda h: bias_acc[h, :HALF, :] + bias_acc[h, HALF:, :], flat, src3)
            core_copy(3).start()
            add_core(2)
            add_x(1)
            gather_z(0)


    add_core(4)
    add_core(3)

    @pl.loop(0, LEVELS)
    def _(zz):
        lev = (zz + 1) % LEVELS
        w, zl = zz // 2, zz % 2
        for g in range(3):
            for lp in range(12 if g < 2 else 6):
                at, r = lp * 6, 12 * g + lp
                tiles[lev, r, 3:9, :] = win[0, w, g, 0, zl, at : at + 6, :]
                tiles[lev, r, 9:12, :] = win[0, w, g, 1, zl, at : at + 3, :]
                pack32[lev, r * 3 : r * 3 + 3, 0:WIDTH] = win[0, w, g, 1, zl, at + 3 : at + 6, :]
        d_send[lev] = pack32[lev, :, 0:WIDTH].astype(BF16)
        for r in range(6):
            pack32[lev, r * 12 : r * 12 + 12, 0:WIDTH] = tiles[lev, r]
        e_send[lev] = pack32[lev, 0:80, 0:WIDTH].astype(BF16)

    d_copy = remote(d_send, d_recv, halo_send.at[3], halo_recv.at[3], (lat, east))
    e_copy = remote(e_send, e_recv, halo_send.at[4], halo_recv.at[4], (up, lon))
    f_copy = remote(d_send.at[:, 0:32], f_recv, halo_send.at[5], halo_recv.at[5], (up, east))
    d_copy.start()

    @pl.when(lat > 0)
    def _():
        e_copy.start()
        f_copy.start()

    add_x(2)
    gather_z(1)
    gather_x(0)
    add_x(4)
    add_x(3)
    gather_z(2)
    gather_x(1)
    gather_core(0)
    lat_send_buf[...] = add_z(4)
    lat_buf[lat] = lat_send_buf[...]
    start(lat_copies)
    gather_z(3)
    gather_x(2)
    gather_core(1)
    wait(lat_copies)
    total = lat_buf[0].astype(F32)
    for i in range(1, LATS):
        total = total + lat_buf[i].astype(F32)
    outs[4][mine] = total.astype(BF16)
    start(gz_copies(4))
    gather_x(3)
    gather_core(2)
    finish(0)

    d_copy.wait()

    @pl.when(lat > 0)
    def _():
        e_copy.wait_send()
        f_copy.wait_send()

    @pl.when(lat < LATS - 1)
    def _():
        e_copy.wait_recv()
        f_copy.wait_recv()

    column = lax.broadcasted_iota(jnp.int32, (COLS, WIDTH), 0)

    @pl.loop(0, LEVELS)
    def _(lev):
        pack32[lev, :, 0:WIDTH] = d_recv[lev].astype(F32)
        corner32[lev, :, 0:WIDTH] = f_recv[lev].astype(F32)
        for row in range(ROWS):
            if row < 18:
                own = tiles[lev, row + 6]
                from_west = pack32[lev, (row + 6) * 3 : (row + 6) * 3 + 3, 0:WIDTH]
            else:
                r = row - 18
                own = jnp.where(last, tiles[lev, 24 + r], e_recv[lev, r * 12 : r * 12 + 12, :].astype(F32))
                from_west = jnp.where(
                    last,
                    pack32[lev, (24 + r) * 3 : (24 + r) * 3 + 3, 0:WIDTH],
                    corner32[lev, r * 3 : r * 3 + 3, 0:WIDTH],
                )
            from_west = jnp.concatenate([from_west, jnp.zeros((COLS - 3, WIDTH), F32)], axis=0)
            cells_out[lev, row] = jnp.where(column < 3, from_west, own).astype(BF16)

    cells_store = pltpu.make_async_copy(cells_out, input_grad_hbm, local_sem.at[7])
    cells_store.start()
    gather_x(4)
    gather_core(3)
    finish(1)
    gather_core(4)
    finish(2)
    finish(3)
    gc_copy(4).wait()
    unfold_weights(outs[4], weight_acc, qkv_grad_ref, out_grad_ref, gain_grad_ref)
    for c in range(4):
        bias_store(c).wait()
    cells_store.wait()


def block(fields, out_grad, gain, qkv, out_weight, bias):
    dma = pltpu.SemaphoreType.DMA
    vmem = pl.BlockSpec(memory_space=pltpu.VMEM)
    hbm = pl.BlockSpec(memory_space=pl.ANY)

    def per_chunk(count):
        return [pltpu.VMEM((count, rows, 128), BF16) for rows in CHUNK_ROWS]

    return pl.pallas_call(
        kernel,
        out_shape=(
            jax.ShapeDtypeStruct((LEVELS, ROWS, COLS, WIDTH), BF16),
            jax.ShapeDtypeStruct((WIDTH, 3 * WIDTH), F32),
            jax.ShapeDtypeStruct((WIDTH, WIDTH), F32),
            jax.ShapeDtypeStruct((1, WIDTH), F32),
            jax.ShapeDtypeStruct((2, 2, HEADS, TOKENS, TOKENS), F32),
        ),
        in_specs=[hbm, hbm, vmem, vmem, vmem, vmem, hbm],
        out_specs=(hbm, vmem, vmem, vmem, hbm),
        scratch_shapes=[
            pltpu.VMEM((LEVELS, ROWS, COLS, WIDTH), BF16),
            pltpu.VMEM((LEVELS, ROWS, COLS, WIDTH), BF16),
            pltpu.VMEM((2, 2, HEADS, TOKENS, TOKENS), F32),
            pltpu.VMEM((2, 2, HEADS, TOKENS, TOKENS), F32),
            pltpu.VMEM((LEVELS, ROWS, COLS, WIDTH), BF16),
            pltpu.VMEM((LEVELS, 80, 2 * WIDTH), BF16),
            pltpu.VMEM((LEVELS, 80, 2 * WIDTH), BF16),
            pltpu.VMEM((LEVELS, 80, 2 * WIDTH), BF16),
            pltpu.VMEM((LEVELS, 80, 2 * WIDTH), BF16),
            pltpu.VMEM((LEVELS, 32, 2 * WIDTH), BF16),
            pltpu.VMEM((LEVELS, 96, 2 * WIDTH), F32),
            pltpu.VMEM((LEVELS, 80, 2 * WIDTH), F32),
            pltpu.VMEM((LEVELS, 32, 2 * WIDTH), F32),
            pltpu.VMEM((2, 2, 3, 2, 2, HALF, WIDTH), F32),
            pltpu.VMEM((HEADS, TOKENS, TOKENS), F32),
            pltpu.VMEM((HEADS, TOKENS, TOKENS), F32),
            pltpu.VMEM((4 * WIDTH, WIDTH), F32),
            pltpu.VMEM((1, WIDTH), F32),
            pltpu.VMEM((1024, 128), F32),
            pltpu.VMEM((LEVELS, 30, COLS, WIDTH), F32),
            pltpu.VMEM((LEVELS, 80, WIDTH), BF16),
            pltpu.VMEM((LEVELS, 96, WIDTH), BF16),
            pltpu.VMEM((LEVELS, 80, WIDTH), BF16),
            pltpu.VMEM((LEVELS, 96, WIDTH), BF16),
            pltpu.VMEM((LEVELS, 32, WIDTH), BF16),
            *per_chunk(LONS),
            *per_chunk(16),
            *per_chunk(8),
            *per_chunk(Z - 1),
            *per_chunk(LONS),
            pltpu.VMEM((48, 128), BF16),
            pltpu.VMEM((LATS, 48, 128), BF16),
            dma((8,)), dma((6,)), dma((6,)), dma((5, 4)), dma((5, 4)),
            dma((5, Z - 1)), dma((5, Z - 1)), dma((5, Z - 1)), dma((5, Z - 1)),
            dma((LATS - 1,)), dma((LATS - 1,)),
        ],
        compiler_params=pltpu.CompilerParams(
            vmem_limit_bytes=VMEM_LIMIT, collective_id=0, has_side_effects=True
        ),
        name="block",
    )(fields, out_grad, gain.reshape(1, WIDTH), qkv, qkv.T, out_weight, bias)


def local(fields, out_grad, gain, qkv_weight, out_weight, window_bias):
    tables = window_bias.reshape(2, 2, HEADS, TOKENS, TOKENS)
    input_grad, qkv_grad, out_weight_grad, gain_grad, bias = block(
        fields, out_grad, gain, qkv_weight, out_weight, tables
    )
    return (
        input_grad,
        qkv_grad,
        out_weight_grad,
        gain_grad.reshape(WIDTH),
        bias.reshape(2, 2, HEADS, TOKENS * TOKENS),
    )


def solution(mesh):
    in_specs = (
        P(None, "lat", "lon", None),
        P(None, "lat", "lon", None),
        P(),
        P(),
        P(),
        P("lat", None, None, None),
    )
    out_specs = (P(None, "lat", "lon", None), P(), P(), P(), P("lat", None, None, None))
    return jax.shard_map(local, mesh=mesh, in_specs=in_specs, out_specs=out_specs, check_vma=False)
```

time: 734 us -> 97.1 us (0.13)
  waiting for transfers between devices: 375 us -> 0 us
  local copies, waits for them, and re-layouts: 140 us -> 22.6 us
  blocking collectives: 83.7 us -> 0 us
  Pallas kernels: 0 us -> 73.5 us
  matrix products: 59 us -> 0 us
  other arithmetic: 40.6 us -> 0 us
  starting transfers between devices: 16.6 us -> 0 us
  between operations: 14.4 us -> 0.68 us
    psum x2 -> x0, waiting for transfers between devices: 368 us -> none  [the longest x1 229 us: local(): bias_total = lax.psum(bias_flat, 'lon')]
    psum x1 -> x0, blocking collectives: 83.7 us -> none  [local(): lax.psum((qkv_sum, out_sum, gain_part), ('lat', 'lon'))]
    pallas_call x0 -> x1, Pallas kernels: none -> 73.5 us  [block(): pl.pallas_call(kernel, out_shape=(jax.ShapeDtypeStruct((LEVELS, ROWS, COL...]
    reshape x42 -> x4, local copies, waits for them, and re-layouts: 60.3 us -> 12.4 us  [the longest x2 6.38 us: local(): tables = window_bias.reshape(2, 2, HEADS, TOKENS, TOKENS)]
    dot_general x30 -> x0, matrix products: 47.4 us -> none  [the longest x3 6.15 us: window_row(): out_part = jnp.dot(attended.T, upstream, preferred_element_type=f32)]
    dynamic_slice x9 -> x0, local copies, waits for them, and re-layouts: 16.8 us -> none  [local(): lax.scan(visit, start, (stack_rows(shifted_in), stack_rows(shifted_grad),...]
    ppermute x6 -> x0, starting transfers between devices: 16.5 us -> none  [the longest x3 9.34 us: from_behind(): return lax.ppermute(block, axis, route)]
    reduce_sum x9 -> x0, other arithmetic: 16.3 us -> none  [the longest x3 9.95 us: window_row(): bias_part = jnp.sum(grad_scores, axis=1)]
  transfers between devices with their start and end apart: 8 -> 0, of which waited for: 4 -> 0; matrix products, arithmetic and copies ran while one was open for 5% -> 0% of each run, Pallas kernels for 0% -> 0%
where the time goes in v2:
time: 97.1 us; the launch traced here: 96.8 us
  Pallas kernels  73.5 us (76%)
  local copies, waits for them, and re-layouts  22.6 us (23%)
    pallas_call x1, Pallas kernels, block(): pl.pallas_call(kernel, out_shape=(jax.ShapeDtypeStruct((LEVELS, ROWS, COL...  73.5 us
    unnamed x13, local copies, waits for them, and re-layouts  10.1 us
    reshape x2, local copies, waits for them, and re-layouts, local(): tables = window_bias.reshape(2, 2, HEADS, TOKENS, TOKENS)  6.38 us
    reshape x2, local copies, waits for them, and re-layouts, local(): bias.reshape(2, 2, HEADS, TOKENS * TOKENS)  6.05 us

profile of v2, /device:TPU:1, one launch (start us, length us, event | category | flops | bytes accessed | tf_op | source)
XLA Modules:
  0.0 96.8 jit_solution(2372294925286561960)
XLA Ops:
  0.6 1.8 %copy.17 = bf16[192,576]{0,1:T(8,128)(2,1)} copy(bf16[192,576]{1,0:T(8,128)(2,1)} %qkv_ref.1) | data formatting | bytes 442368 | tf_op args[3]
  2.4 2.1 %copy.18.fields_hbm = bf16[4,24,12,192]{3,2,1,0:T(8,128)(2,1)} copy(bf16[4,24,12,192]{3,1,2,0:T(8,128)(2,1)} %param.6) | data formatting | bytes 884736 | tf_op args[0]
  4.5 2.1 %copy.19.grad_hbm = bf16[4,24,12,192]{3,2,1,0:T(8,128)(2,1)} copy(bf16[4,24,12,192]{3,1,2,0:T(8,128)(2,1)} %param.7) | data formatting | bytes 884736 | tf_op args[1]
  6.6 4.3 %reshape.23 = f32[2,2,6,144,144]{4,3,1,2,0:T(8,128)S(1)} reshape(f32[2,2,6,20736]{3,1,2,0:T(2,128)} %param.11) | data formatting | bytes 3981312 | tf_op jit(solution)/shard_map/reshape | solution.py:621
  10.9 2.0 %copy.20.bias_hbm = f32[2,2,6,144,144]{4,3,2,1,0:T(8,128)} copy(f32[2,2,6,144,144]{4,3,1,2,0:T(8,128)S(1)} %reshape.23) | data formatting | bytes 3981312 | tf_op jit(solution)/shard_map/reshape | solution.py:621
  13.0 73.5 %block.1 = (bf16[4,24,12,192]{3,2,1,0:T(8,128)(2,1)}, f32[192,576]{1,0:T(8,128)}, f32[192,192]{1,0:T(8,128)}, f32[1,192]{1,0:T(1,128)}, f32[2,2,6,144,144]{4,3,2,1,0:T(8,128)}) custom-call(bf16[4,24,12,192]{3,2,1,0:T(8,128)(2,1)} %copy.18.fields_hbm, bf16[4,24,12,192]{3,2,1,0:T(8,128)(2,1)} %copy.19.grad_hbm, f32[1,192]{1,0:T(1,128)} %bitcast.8, ...), custom_call_target="tpu_custom_call" | custom-call | tf_op jit(solution)/shard_map/block/pallas_call | solution.py:565
  86.5 2.1 %copy.22 = bf16[4,24,12,192]{3,1,2,0:T(8,128)(2,1)} copy(bf16[4,24,12,192]{3,2,1,0:T(8,128)(2,1)} %get-tuple-element.20) | data formatting | bytes 884736
  88.7 3.7 %reshape.26 = f32[2,2,6,20736]{3,2,1,0:T(8,128)S(1)} reshape(f32[2,2,6,144,144]{4,3,2,1,0:T(8,128)} %get-tuple-element.14) | data formatting | bytes 3981312 | tf_op jit(solution)/shard_map/reshape | solution.py:630
  92.4 0.0 copy-start
  92.4 0.0 copy-start.1
  92.4 0.0 copy-start.2
  92.4 2.3 %copy.23 = f32[2,2,6,20736]{3,1,2,0:T(2,128)} copy(f32[2,2,6,20736]{3,2,1,0:T(8,128)S(1)} %reshape.26) | data formatting | bytes 3981312 | tf_op jit(solution)/shard_map/reshape | solution.py:630
  94.7 0.0 copy-done
  94.7 0.8 copy.27
  95.5 0.0 copy-done.1
  95.5 0.7 copy.28
  96.2 0.0 copy-done.2
  96.2 0.6 copy.29
Async XLA Ops:
  92.4 2.3 %copy-start = (f32[192,576]{1,0:T(8,128)S(1)}, f32[192,576]{1,0:T(8,128)}, u32[]{:S(2)}) copy-start(f32[192,576]{1,0:T(8,128)} %get-tuple-element.31) | copy-start | bytes 1327108
  92.4 3.1 %copy-start.1 = (f32[192,192]{1,0:T(8,128)S(1)}, f32[192,192]{1,0:T(8,128)}, u32[]{:S(2)}) copy-start(f32[192,192]{1,0:T(8,128)} %get-tuple-element.32) | copy-start | bytes 442372
  92.4 3.8 %copy-start.2 = (f32[1,192]{1,0:T(1,128)S(1)}, f32[1,192]{1,0:T(1,128)}, u32[]{:S(2)}) copy-start(f32[1,192]{1,0:T(1,128)} %get-tuple-element.13) | copy-start | bytes 2308

commit v3 on v2

v3 whole, which is shorter than its diff:
```python
import jax
import jax.numpy as jnp
from jax import lax
from jax.experimental import pallas as pl
from jax.experimental.layout import Layout, with_layout_constraint
from jax.experimental.pallas import tpu as pltpu
from jax.sharding import PartitionSpec as P

F32 = jnp.float32
BF16 = jnp.bfloat16
MESH = pl.DeviceIdType.MESH

EPS = 1e-05
MASKED = -1e30
LOG2E = 1.4426950408889634

LEVELS = 4
ROWS = 24
COLS = 12
WIDTH = 192
HEADS = 6
HEAD = 32
TOKENS = 144
HALF = 72
FLAT = 162
LATS = 8
LONS = 32
Z = 8

CHUNK_ROWS = (32, 16, 32, 16, 48)
BIAS_CHUNKS = ((1, 0), (1, 1), (0, 0), (0, 1))
WEIGHTS = 4

VMEM_LIMIT = 56 * 1024 * 1024


def dot(a, b, contract=(1, 0)):
    return lax.dot_general(
        a, b, (((contract[0],), (contract[1],)), ((), ())), preferred_element_type=F32
    )


def remote(source, target, send, recv, there):
    return pltpu.make_async_remote_copy(
        src_ref=source, dst_ref=target, send_sem=send, recv_sem=recv, device_id=there, device_id_type=MESH
    )


def place_of(c):
    return c // 6, c % 6


def put_rows(win, at, start, rows):
    k, w, g, n, zl = at
    count = rows.shape[0]
    where_to = pl.ds(start, count, stride=6)
    win[k, w, g, n, 0, zl, where_to, :] = rows[:, :128]
    win[k, w, g, n, 1, zl, where_to, :] = jnp.concatenate([rows[:, 128:], jnp.zeros((count, 64), F32)], axis=1)


def take_rows(win, at, start, count):
    k, w, g, n, zl = at
    where_from = pl.ds(start, count, stride=6)
    return jnp.concatenate(
        [win[k, w, g, n, 0, zl, where_from, :], win[k, w, g, n, 1, zl, where_from, :][:, :64]], axis=1
    )


def take_window(win, at):
    return jnp.concatenate(
        [win[(*at, 0)].reshape(TOKENS, 128), win[(*at, 1)].reshape(TOKENS, 128)[:, :64]], axis=1
    )


def put_cells(own, win, k):
    @pl.loop(0, LEVELS)
    def _(z):
        lev, w, zl = (z + 1) % LEVELS, z // 2, z % 2
        for c in range(9):
            n, lo = place_of(c)
            tile = own[lev, c + 3].astype(F32)
            put_rows(win, (k, w, 0, n, zl), 36 + lo, tile[0:6])
            put_rows(win, (k, w, 1, n, zl), lo, tile[6:18])
            put_rows(win, (k, w, 2, 0, zl), 36 * n + lo, tile[18:24])


def put_east(east, win, k):
    @pl.loop(0, LEVELS)
    def _(z):
        lev, w, zl = (z + 1) % LEVELS, z // 2, z % 2
        for j in range(3):
            n, lo = place_of(9 + j)
            tile = east[k, lev, j].astype(F32)
            put_rows(win, (k, w, 0, n, zl), 36 + lo, tile[0:6])
            put_rows(win, (k, w, 1, n, zl), lo, tile[6:18])
            put_rows(win, (k, w, 2, 0, zl), 36 * n + lo, tile[18:24])


def put_above(above, corner, above32, corner32, win, lat):
    @pl.loop(0, LEVELS)
    def _(z):
        lev, w, zl = (z + 1) % LEVELS, z // 2, z % 2
        above32[lev, 0:64] = jnp.where(lat == 0, 0.0, above[lev].astype(F32))
        corner32[lev] = jnp.where(lat == 0, 0.0, corner[lev].astype(F32))
        for k in range(2):
            lanes = slice(k * WIDTH, (k + 1) * WIDTH)
            for c in range(12):
                n, lo = place_of(c)
                if c < 9:
                    cells = above32[lev, c * 6 : c * 6 + 6, lanes]
                else:
                    cells = corner32[lev, (c - 9) * 6 : (c - 9) * 6 + 6, lanes]
                put_rows(win, (k, w, 0, n, zl), lo, cells)


def window(win, w, g, n, gain, qkv_ref, query_t_ref, out_ref, masked, bias_acc, weight_acc, gain_acc):
    masked_lo, masked_hi = masked
    acc_lo, acc_hi = bias_acc
    scale = HEAD ** (-0.5)
    x = take_window(win, (0, w, g, n))
    centred = x - jnp.mean(x, axis=-1, keepdims=True)
    inv_std = lax.rsqrt(jnp.mean(centred * centred, axis=-1, keepdims=True) + EPS)
    standard = centred * inv_std
    normed = (standard * gain).astype(BF16)
    upstream32 = take_window(win, (1, w, g, n))
    upstream = upstream32.astype(BF16)
    projected = dot(normed, qkv_ref[...]).astype(BF16)
    queries_t = dot(query_t_ref[...], normed, (1, 1)).astype(BF16)
    attended_grad = dot(upstream, out_ref[...], (1, 1)).astype(BF16)
    attended_grad_t = dot(out_ref[...], upstream, (1, 1)).astype(BF16)
    lane = lax.broadcasted_iota(jnp.int32, (TOKENS, WIDTH), 1)
    own = [(lane // HEAD) == h for h in range(HEADS)]
    zero = jnp.zeros((), BF16)
    queries_all = jnp.concatenate([jnp.where(own[h], projected[:, :WIDTH], zero) for h in range(HEADS)], axis=0)
    upper_all = jnp.concatenate([jnp.where(own[h], attended_grad, zero) for h in range(HEADS)], axis=0)
    keys = projected[:, WIDTH : 2 * WIDTH]
    values = projected[:, 2 * WIDTH :]
    scores_all = dot(queries_all, keys, (1, 1))
    grads_all = dot(upper_all, values, (1, 1))
    keys_parts, values_parts, lows, scores_lows = [], [], [], []
    for h in range(HEADS):
        at = slice(h * TOKENS, (h + 1) * TOKENS)
        rows = slice(h * HEAD, (h + 1) * HEAD)
        table = jnp.concatenate([masked_lo[h], masked_hi[h, :, :16]], axis=1)
        scores = scores_all[at] * (scale * LOG2E) + table
        exps = jnp.exp2(scores - jnp.max(scores, axis=-1, keepdims=True))
        attention = exps * (1.0 / jnp.sum(exps, axis=-1, keepdims=True))
        low = attention.astype(BF16)
        attention_grad = grads_all[at]
        delta = jnp.sum(attention * attention_grad, axis=-1, keepdims=True)
        scores_grad = attention * (attention_grad - delta)
        acc_lo[h] += scores_grad[:, :128]
        acc_hi[h, :, :16] += scores_grad[:, 128:]
        scores_low = scores_grad.astype(BF16)
        lows.append(low)
        scores_lows.append(scores_low)
        values_parts.append(dot(attended_grad_t[rows], low).astype(BF16))
        keys_parts.append((dot(queries_t[rows], scores_low) * scale).astype(BF16))
    attended_all = dot(jnp.concatenate(lows, axis=0), values)
    queries_grad_all = dot(jnp.concatenate(scores_lows, axis=0), keys)
    attended_sum = jnp.zeros((TOKENS, WIDTH), F32)
    queries_sum = jnp.zeros((TOKENS, WIDTH), F32)
    for h in range(HEADS):
        at = slice(h * TOKENS, (h + 1) * TOKENS)
        attended_sum = jnp.where(own[h], attended_all[at], attended_sum)
        queries_sum = jnp.where(own[h], queries_grad_all[at], queries_sum)
    attended_t = jnp.transpose(attended_sum).astype(BF16)
    queries_grad_t = (jnp.transpose(queries_sum) * scale).astype(BF16)
    projected_grad_t = jnp.concatenate([queries_grad_t] + keys_parts + values_parts, axis=0)
    weight_acc[3 * WIDTH :, :] += dot(attended_t, upstream)
    weight_acc[: 3 * WIDTH, :] += dot(projected_grad_t, normed)
    shifted_t = dot(qkv_ref[...], projected_grad_t)
    grad = jnp.transpose(shifted_t).astype(BF16).astype(F32)
    product = grad * standard
    gain_acc[...] += jnp.sum(product, axis=0, keepdims=True)
    scaled = grad * gain
    ig = upstream32 + inv_std * (
        scaled
        - jnp.mean(scaled, axis=-1, keepdims=True)
        - standard * jnp.mean(product * gain, axis=-1, keepdims=True)
    )
    win[0, w, g, n, 0] = ig[:, :128].reshape(2, HALF, 128)
    win[0, w, g, n, 1, :, :, 0:64] = ig[:, 128:].reshape(2, HALF, 64)


def mask_bias(masked, bias_ref, w, g, lat):
    masked_lo, masked_hi = masked
    table = jnp.minimum(g, 1)
    lane = lax.broadcasted_iota(jnp.int32, (18, 128), 1)

    def low(token):
        return (token // 6) % 12 < 6

    for i in range(8):
        q = 8 * lax.broadcasted_iota(jnp.int32, (18, 1), 0) + i

        def blocked(k):
            half = ((q >= HALF) != (k >= HALF)) & (w == 1)
            top = (low(q) | low(k)) & (g == 0) & (lat == 0)
            bottom = (low(q) != low(k)) & (g == 2)
            return half | top | bottom

        k = lax.broadcasted_iota(jnp.int32, (1, 128), 1)
        blocked_lo, blocked_hi = blocked(k), blocked(k + 128)
        for h in range(HEADS):
            at = (table * HEADS + h) * (2 * FLAT) + w + 2 * i
            first = bias_ref[pl.ds(at, 18, stride=18), :]
            second = bias_ref[pl.ds(at + 2, 18, stride=18), :]
            lo = jnp.where(lane >= 16 * i, first, second)
            hi = second
            if i:
                lo = pltpu.roll(lo, 128 - 16 * i, 1)
                hi = pltpu.roll(hi, 128 - 16 * i, 1)
            masked_lo[h, pl.ds(i, 18, stride=8), :] = jnp.where(blocked_lo, MASKED, lo * LOG2E)
            masked_hi[h, pl.ds(i, 18, stride=8), :] = jnp.where(blocked_hi, MASKED, hi * LOG2E)


def double_mask(masked):
    masked_lo, masked_hi = masked
    k = lax.broadcasted_iota(jnp.int32, (36, 128), 1)
    own = (k // 6) % 12 >= 6
    for h in range(HEADS):
        for at in (0, HALF):
            rows = pltpu.roll(masked_lo[h, at : at + 36, :], 36, 1)
            masked_lo[h, at + 36 : at + 72, :] = jnp.where(own, rows, MASKED)
            masked_hi[h, at + 36 : at + 72, :] = rows


def join_sums(bias_acc):
    acc_lo, acc_hi = bias_acc
    lane = lax.broadcasted_iota(jnp.int32, (36, 128), 1)
    for h in range(HEADS):
        for at in (0, HALF):
            second = slice(at + 36, at + 72)
            lo, hi = pltpu.roll(acc_lo[h, second, :], 92, 1), pltpu.roll(acc_hi[h, second, :], 92, 1)
            acc_lo[h, at : at + 36, :] += jnp.where(lane < 92, lo, hi)
            acc_lo[h, second, :] = jnp.zeros((36, 128), F32)
            acc_hi[h, second, :] = jnp.zeros((36, 128), F32)


def fold(w, bias_acc, flat, src):
    acc_lo, acc_hi = bias_acc
    groups = (18, 9)[w]
    lane = lax.broadcasted_iota(jnp.int32, (groups, 128), 1)

    def take(ref, h, i):
        value = ref[h, pl.ds(i, groups, stride=8), :]
        return value + ref[h, pl.ds(HALF + i, groups, stride=8), :] if w else value

    for h in range(HEADS):
        before_lo = before_hi = None
        for i in range(9):
            if i < 8:
                lo, hi = take(acc_lo, h, i), take(acc_hi, h, i)
                if i:
                    lo, hi = pltpu.roll(lo, 16 * i, 1), pltpu.roll(hi, 16 * i, 1)
            rows = lo
            if i:
                rows = jnp.where(lane >= 16 * (i - 1), before_hi, before_lo)
                if i < 8:
                    rows = jnp.where(lane >= 16 * i, lo, rows)
            flat[pl.ds(h * 9 * groups + i, groups, stride=9), :] = rows
            before_lo, before_hi = lo, hi
    each = (32, 16)[w]
    flat[HEADS * 9 * groups : LONS * each, :] = jnp.zeros((LONS * each - HEADS * 9 * groups, 128), F32)
    src[...] = flat[: LONS * each, :].astype(BF16).reshape(LONS, each, 128)


def fold_weights(weight_acc, gain_acc, src):
    for s in range(16):
        src[s] = weight_acc[s * 48 : (s + 1) * 48, :128].astype(BF16)
    for s in range(8):
        pair = jnp.concatenate(
            [weight_acc[s * 48 : (s + 1) * 48, 128:], weight_acc[384 + s * 48 : 384 + (s + 1) * 48, 128:]], axis=1
        )
        src[16 + s] = pair.astype(BF16)
    total = gain_acc[...]
    left = jnp.broadcast_to(total[:, :128], (48, 128))
    right = jnp.concatenate([total[:, 128:], jnp.zeros((1, 64), F32)], axis=1)
    right = jnp.broadcast_to(right, (48, 128))
    row = lax.broadcasted_iota(jnp.int32, (48, 128), 0)
    src[24] = jnp.where(row == 0, left, jnp.where(row == 1, right, 0.0)).astype(BF16)
    src[25:] = jnp.zeros((LONS - 25, 48, 128), BF16)


def unfold(g, w, out, flat, bias_out):
    each = (32, 16)[w]
    flat[: LONS * each, :] = out[...].reshape(LONS * each, 128).astype(F32)
    row = lax.broadcasted_iota(jnp.int32, (81, 128), 0)
    lane = lax.broadcasted_iota(jnp.int32, (81, 128), 1)
    left = (128 * row + lane) % TOKENS < HALF
    for h in range(HEADS):
        at = (g * HEADS + h) * (2 * FLAT) + w
        if w == 0:
            bias_out[pl.ds(at, FLAT, stride=2), :] = flat[h * FLAT : (h + 1) * FLAT, :]
        else:
            rows = flat[h * 81 : (h + 1) * 81, :]
            bias_out[pl.ds(at, 81, stride=2), :] = jnp.where(left, rows, 0.0)
            bias_out[pl.ds(at + FLAT, 81, stride=2), :] = jnp.where(left, 0.0, rows)


def unfold_weights(out, weight, qkv_ref, out_ref, gain_ref):
    for s in range(16):
        weight[s * 48 : (s + 1) * 48, :128] = out[s].astype(F32)
    for s in range(8):
        pair = out[16 + s].astype(F32)
        weight[s * 48 : (s + 1) * 48, 128:] = pair[:, :64]
        weight[384 + s * 48 : 384 + (s + 1) * 48, 128:] = pair[:, 64:]
    gain = out[24, 0:16, :].astype(F32)
    gain_ref[:, :128] = gain[0:1, :]
    gain_ref[:, 128:] = gain[1:2, :64]
    qkv_ref[...] = jnp.transpose(weight[: 3 * WIDTH, :])
    out_ref[...] = weight[3 * WIDTH :, :]


def kernel(
    fields_hbm, grad_hbm, gain_ref, qkv_ref, out_w_ref, bias_hbm,
    input_grad_hbm, qkv_grad_ref, out_grad_ref, gain_grad_ref, bias_grad_hbm,
    fields, grads, bias, bias_out, cells_out, query_t,
    a_send, a_recv, b_recv, c_recv, pack32, corner32,
    win, masked_lo, masked_hi, acc_lo, acc_hi, weight_acc, gain_acc, flat,
    tiles, d_send, e_send, d_recv, e_recv, f_recv,
    src0, src1, src2, src3, src4, core0, core1, core2, core3, core4,
    xb0, xb1, xb2, xb3, xb4, zb0, zb1, zb2, zb3, zb4, out0, out1, out2, out3, out4,
    lat_send_buf, lat_buf,
    local_sem, halo_send, halo_recv, pair_send, pair_recv, z_send, z_recv, gz_send, gz_recv, lat_send, lat_recv,
):
    masked, bias_acc = (masked_lo, masked_hi), (acc_lo, acc_hi)
    lat = lax.axis_index("lat")
    lon = lax.axis_index("lon")
    last = lat == LATS - 1
    z, x, core = lon // 4, (lon // 2) % 2, lon % 2
    up, down = (lat + LATS - 1) % LATS, (lat + 1) % LATS
    west, east = (lon + LONS - 1) % LONS, (lon + 1) % LONS

    def at_lon(zz, xx, cc):
        return (lat, zz * 4 + xx * 2 + cc)

    core_peer = at_lon(z, x, 1 - core)
    x_peer = at_lon(z, 1 - x, core)
    z_peers = [at_lon((z + d) % Z, x, core) for d in range(1, Z)]
    lat_peers = [((lat + d) % LATS, lon) for d in range(1, LATS)]

    loads = [
        pltpu.make_async_copy(fields_hbm, fields, local_sem.at[0]),
        pltpu.make_async_copy(grad_hbm, grads, local_sem.at[1]),
        pltpu.make_async_copy(bias_hbm, bias, local_sem.at[2]),
    ]
    for c in loads:
        c.start()
    barrier = pltpu.get_barrier_semaphore()
    greeted = [core_peer, x_peer, (lat, west), (lat, east), (down, west), (up, east)] + z_peers + lat_peers
    for there in greeted:
        pl.semaphore_signal(barrier, inc=1, device_id=there, device_id_type=MESH)

    loads[0].wait()
    loads[1].wait()

    @pl.loop(0, LEVELS)
    def _(lev):
        for k, own in enumerate((fields, grads)):
            for col in range(COLS):
                at = (col - 3) * 6 if col >= 3 else 64 + col * 6
                pack32[lev, at : at + 6, k * WIDTH : (k + 1) * WIDTH] = own[lev, col].astype(F32)[18:24]
        a_send[lev] = pack32[lev].astype(BF16)

    pl.semaphore_wait(barrier, len(greeted))
    b_copies = [
        remote(own.at[:, 0:3], b_recv.at[k], halo_send.at[k], halo_recv.at[k], (lat, west))
        for k, own in enumerate((fields, grads))
    ]
    a_copy = remote(a_send.at[:, 0:64], a_recv, halo_send.at[2], halo_recv.at[2], (down, lon))
    c_copy = remote(a_send.at[:, 64:96], c_recv, halo_send.at[3], halo_recv.at[3], (down, west))
    for c in b_copies:
        c.start()

    @pl.when(lat < LATS - 1)
    def _():
        a_copy.start()
        c_copy.start()

    weight_acc[...] = jnp.zeros_like(weight_acc)
    gain_acc[...] = jnp.zeros_like(gain_acc)
    query_t[...] = jnp.transpose(qkv_ref[:, :WIDTH].astype(F32)).astype(BF16)
    for k, own in enumerate((fields, grads)):
        put_cells(own, win, k)
    loads[2].wait()
    for c in b_copies:
        c.wait()
    for k in range(2):
        put_east(b_recv, win, k)

    srcs = (src0, src1, src2, src3, src4)
    core_bufs = (core0, core1, core2, core3, core4)
    x_bufs = (xb0, xb1, xb2, xb3, xb4)
    z_bufs = (zb0, zb1, zb2, zb3, zb4)
    outs = (out0, out1, out2, out3, out4)
    mine = core * 16 + x * 8 + z

    def core_copy(c):
        return remote(
            srcs[c].at[pl.ds((1 - core) * 16, 16)], core_bufs[c], pair_send.at[c, 0], pair_recv.at[c, 0], core_peer
        )

    def x_copy(c):
        return remote(
            srcs[c].at[pl.ds(core * 16 + (1 - x) * 8, 8)], x_bufs[c], pair_send.at[c, 1], pair_recv.at[c, 1], x_peer
        )

    def z_copies(c):
        return [
            remote(
                srcs[c].at[core * 16 + x * 8 + (z + d) % Z], z_bufs[c].at[d - 1],
                z_send.at[c, d - 1], z_recv.at[c, d - 1], z_peers[d - 1],
            )
            for d in range(1, Z)
        ]

    def gz_copies(c):
        part = outs[c].at[mine]
        return [remote(part, part, gz_send.at[c, d - 1], gz_recv.at[c, d - 1], z_peers[d - 1]) for d in range(1, Z)]

    def gx_copy(c):
        part = outs[c].at[pl.ds(core * 16 + x * 8, 8)]
        return remote(part, part, pair_send.at[c, 2], pair_recv.at[c, 2], x_peer)

    def gc_copy(c):
        part = outs[c].at[pl.ds(core * 16, 16)]
        return remote(part, part, pair_send.at[c, 3], pair_recv.at[c, 3], core_peer)

    lat_copies = [
        remote(lat_send_buf, lat_buf.at[lat], lat_send.at[d - 1], lat_recv.at[d - 1], lat_peers[d - 1])
        for d in range(1, LATS)
    ]

    def start(copies):
        for c in copies:
            c.start()

    def wait(copies):
        for c in copies:
            c.wait()

    def add_core(c):
        core_copy(c).wait()
        half = pl.ds(core * 16, 16)
        srcs[c][half] = (srcs[c][half].astype(F32) + core_bufs[c][...].astype(F32)).astype(BF16)
        x_copy(c).start()

    def add_x(c):
        x_copy(c).wait()
        part = pl.ds(core * 16 + x * 8, 8)
        srcs[c][part] = (srcs[c][part].astype(F32) + x_bufs[c][...].astype(F32)).astype(BF16)
        start(z_copies(c))

    def add_z(c):
        wait(z_copies(c))
        total = srcs[c][mine].astype(F32)
        for d in range(Z - 1):
            total = total + z_bufs[c][d].astype(F32)
        return total.astype(BF16)

    def gather_z(c):
        outs[c][mine] = add_z(c)
        start(gz_copies(c))

    def gather_x(c):
        wait(gz_copies(c))
        gx_copy(c).start()

    def gather_core(c):
        gx_copy(c).wait()
        gc_copy(c).start()

    def bias_store(g):
        part = pl.ds(g * 2 * HEADS * FLAT, 2 * HEADS * FLAT)
        return pltpu.make_async_copy(bias_out.at[part], bias_grad_hbm.at[part], local_sem.at[3 + g])

    def finish(c):
        gc_copy(c).wait()
        g, w = BIAS_CHUNKS[c]
        unfold(g, w, outs[c], flat, bias_out)
        if w:
            bias_store(g).start()

    @pl.loop(0, 6)
    def _(t):
        early = jnp.where(t < 4, 1, 0)
        g = early * (2 - t % 2)
        w = early * (t // 2) + (1 - early) * (t - 4)

        @pl.when(t == 4)
        def _():
            @pl.when(lat < LATS - 1)
            def _():
                a_copy.wait_send()
                c_copy.wait_send()

            @pl.when(lat > 0)
            def _():
                a_copy.wait_recv()
                c_copy.wait_recv()

            put_above(a_recv, c_recv, pack32, corner32, win, lat)

        @pl.when((t == 0) | (t == 2) | (t >= 4))
        def _():
            acc_lo[...] = jnp.zeros_like(acc_lo)
            acc_hi[...] = jnp.zeros_like(acc_hi)

        def run(n):
            window(
                win, w, g, n, gain_ref[...], qkv_ref, query_t, out_w_ref, masked, bias_acc, weight_acc, gain_acc
            )

        @pl.when((g == 2) & last)
        def _():
            mask_bias(masked, bias, w, g, lat)
            double_mask(masked)
            run(0)
            join_sums(bias_acc)

        @pl.when(g < 2)
        def _():
            mask_bias(masked, bias, w, g, lat)
            run(0)
            run(1)

        @pl.when(t == 1)
        def _():
            fold(0, bias_acc, flat, src0)
            core_copy(0).start()

        @pl.when(t == 3)
        def _():
            fold(1, bias_acc, flat, src1)
            core_copy(1).start()
            add_core(0)

        @pl.when(t == 4)
        def _():
            fold(0, bias_acc, flat, src2)
            core_copy(2).start()
            add_core(1)
            add_x(0)

        @pl.when(t == 5)
        def _():
            fold_weights(weight_acc, gain_acc, src4)
            core_copy(4).start()
            fold(1, bias_acc, flat, src3)
            core_copy(3).start()
            add_core(2)
            add_x(1)
            gather_z(0)


    add_core(4)
    add_core(3)

    @pl.loop(0, LEVELS)
    def _(zz):
        lev, w, zl = (zz + 1) % LEVELS, zz // 2, zz % 2
        for c in range(COLS):
            n, lo = place_of(c)
            col = (c + 3) % COLS
            tiles[lev, col, 0:6, :] = take_rows(win, (0, w, 0, n, zl), 36 + lo, 6)
            tiles[lev, col, 6:18, :] = take_rows(win, (0, w, 1, n, zl), lo, 12)
            tiles[lev, col, 18:24, :] = take_rows(win, (0, w, 2, 0, zl), 36 * n + lo, 6)
            if c >= 9:
                d_send[lev, col] = tiles[lev, col].astype(BF16)
            at = c * 6 if c < 9 else 64 + (c - 9) * 6
            pack32[lev, at : at + 6, 0:WIDTH] = take_rows(win, (0, w, 0, n, zl), lo, 6)
        e_send[lev] = pack32[lev, :, 0:WIDTH].astype(BF16)

    d_copy = remote(d_send, d_recv, halo_send.at[4], halo_recv.at[4], (lat, east))
    e_copy = remote(e_send.at[:, 0:64], e_recv, halo_send.at[5], halo_recv.at[5], (up, lon))
    f_copy = remote(e_send.at[:, 64:96], f_recv, halo_send.at[6], halo_recv.at[6], (up, east))
    d_copy.start()

    @pl.when(lat > 0)
    def _():
        e_copy.start()
        f_copy.start()

    add_x(4)
    add_x(3)
    add_x(2)
    gather_z(1)
    gather_x(0)
    lat_send_buf[...] = add_z(4)
    lat_buf[lat] = lat_send_buf[...]
    start(lat_copies)
    gather_z(3)
    gather_z(2)
    gather_x(1)
    gather_core(0)
    wait(lat_copies)
    total = lat_buf[0].astype(F32)
    for i in range(1, LATS):
        total = total + lat_buf[i].astype(F32)
    outs[4][mine] = total.astype(BF16)
    start(gz_copies(4))
    gather_x(3)
    gather_x(2)
    gather_core(1)
    finish(0)
    gather_x(4)
    finish(1)
    gather_core(3)
    gather_core(2)

    d_copy.wait()

    @pl.when(lat > 0)
    def _():
        e_copy.wait_send()
        f_copy.wait_send()

    @pl.when(lat < LATS - 1)
    def _():
        e_copy.wait_recv()
        f_copy.wait_recv()

    gather_core(4)

    @pl.loop(0, LEVELS)
    def _(lev):
        pack32[lev, 0:64, 0:WIDTH] = e_recv[lev].astype(F32)
        corner32[lev, :, 0:WIDTH] = f_recv[lev].astype(F32)
        for col in range(COLS):
            if col < 3:
                tiles[lev, col] = d_recv[lev, col].astype(F32)
                cells = corner32[lev, col * 6 : col * 6 + 6, 0:WIDTH]
            else:
                cells = pack32[lev, (col - 3) * 6 : (col - 3) * 6 + 6, 0:WIDTH]
            tiles[lev, col, 18:24, :] = jnp.where(last, tiles[lev, col, 18:24, :], cells)
            cells_out[lev, col] = tiles[lev, col].astype(BF16)

    cells_store = pltpu.make_async_copy(cells_out, input_grad_hbm, local_sem.at[7])
    cells_store.start()
    finish(2)
    finish(3)
    gc_copy(4).wait()
    unfold_weights(outs[4], weight_acc, qkv_grad_ref, out_grad_ref, gain_grad_ref)
    for g in range(2):
        bias_store(g).wait()
    cells_store.wait()


def block(fields, out_grad, gain, qkv, out_weight, bias):
    dma = pltpu.SemaphoreType.DMA
    vmem = pl.BlockSpec(memory_space=pltpu.VMEM)
    hbm = pl.BlockSpec(memory_space=pl.ANY)

    def per_chunk(count):
        return [pltpu.VMEM((count, rows, 128), BF16) for rows in CHUNK_ROWS]

    cells = (LEVELS, COLS, ROWS, WIDTH)
    tables = (2 * 2 * HEADS * FLAT, 128)
    return pl.pallas_call(
        kernel,
        out_shape=(
            jax.ShapeDtypeStruct(cells, BF16),
            jax.ShapeDtypeStruct((WIDTH, 3 * WIDTH), F32),
            jax.ShapeDtypeStruct((WIDTH, WIDTH), F32),
            jax.ShapeDtypeStruct((1, WIDTH), F32),
            jax.ShapeDtypeStruct(tables, F32),
        ),
        in_specs=[hbm, hbm, vmem, vmem, vmem, hbm],
        out_specs=(hbm, vmem, vmem, vmem, hbm),
        scratch_shapes=[
            pltpu.VMEM(cells, BF16),
            pltpu.VMEM(cells, BF16),
            pltpu.VMEM(tables, F32),
            pltpu.VMEM(tables, F32),
            pltpu.VMEM(cells, BF16),
            pltpu.VMEM((WIDTH, WIDTH), BF16),
            pltpu.VMEM((LEVELS, 96, 2 * WIDTH), BF16),
            pltpu.VMEM((LEVELS, 64, 2 * WIDTH), BF16),
            pltpu.VMEM((2, LEVELS, 3, ROWS, WIDTH), BF16),
            pltpu.VMEM((LEVELS, 32, 2 * WIDTH), BF16),
            pltpu.VMEM((LEVELS, 96, 2 * WIDTH), F32),
            pltpu.VMEM((LEVELS, 32, 2 * WIDTH), F32),
            pltpu.VMEM((2, 2, 3, 2, 2, 2, HALF, 128), F32),
            pltpu.VMEM((HEADS, TOKENS, 128), F32),
            pltpu.VMEM((HEADS, TOKENS, 128), F32),
            pltpu.VMEM((HEADS, TOKENS, 128), F32),
            pltpu.VMEM((HEADS, TOKENS, 128), F32),
            pltpu.VMEM((4 * WIDTH, WIDTH), F32),
            pltpu.VMEM((1, WIDTH), F32),
            pltpu.VMEM((1024, 128), F32),
            pltpu.VMEM(cells, F32),
            pltpu.VMEM((LEVELS, 3, ROWS, WIDTH), BF16),
            pltpu.VMEM((LEVELS, 96, WIDTH), BF16),
            pltpu.VMEM((LEVELS, 3, ROWS, WIDTH), BF16),
            pltpu.VMEM((LEVELS, 64, WIDTH), BF16),
            pltpu.VMEM((LEVELS, 32, WIDTH), BF16),
            *per_chunk(LONS),
            *per_chunk(16),
            *per_chunk(8),
            *per_chunk(Z - 1),
            *per_chunk(LONS),
            pltpu.VMEM((48, 128), BF16),
            pltpu.VMEM((LATS, 48, 128), BF16),
            dma((8,)), dma((7,)), dma((7,)), dma((5, 4)), dma((5, 4)),
            dma((5, Z - 1)), dma((5, Z - 1)), dma((5, Z - 1)), dma((5, Z - 1)),
            dma((LATS - 1,)), dma((LATS - 1,)),
        ],
        compiler_params=pltpu.CompilerParams(
            vmem_limit_bytes=VMEM_LIMIT, collective_id=0, has_side_effects=True
        ),
        name="block",
    )(fields, out_grad, gain.reshape(1, WIDTH), qkv, out_weight, bias)


def hand_over_kernel(*refs):
    count = (len(refs) - 2) // 3
    sources, targets, held = refs[:count], refs[count : 2 * count], refs[2 * count : 3 * count]
    load_sem, store_sem = refs[-2:]
    loads, stores = [], []
    for k, (source, there, target) in enumerate(zip(sources, held, targets)):
        parts = [None]
        if source.shape[0] == 2 * 2 * HEADS * FLAT:
            parts = [pl.ds(part * 1296, 1296) for part in range(3)]
        elif len(source.shape) == 4:
            parts = [pl.ds(part * 2, 2) for part in range(2)]
        for p, part in enumerate(parts):
            a, b, c = (source, there, target) if part is None else (source.at[part], there.at[part], target.at[part])
            loads.append(pltpu.make_async_copy(a, b, load_sem.at[k, p]))
            stores.append(pltpu.make_async_copy(b, c, store_sem.at[k, p]))
    for c in loads:
        c.start()
    for a, b in zip(loads, stores):
        a.wait()
        b.start()
    for c in stores:
        c.wait()


def hand_over(arrays):
    hbm = pl.BlockSpec(memory_space=pl.ANY)
    dma = pltpu.SemaphoreType.DMA
    return pl.pallas_call(
        hand_over_kernel,
        out_shape=tuple(jax.ShapeDtypeStruct(a.shape, a.dtype) for a in arrays),
        in_specs=[hbm] * len(arrays),
        out_specs=(hbm,) * len(arrays),
        scratch_shapes=[pltpu.VMEM(a.shape, a.dtype) for a in arrays]
        + [dma((len(arrays), 3)), dma((len(arrays), 3))],
        compiler_params=pltpu.CompilerParams(vmem_limit_bytes=VMEM_LIMIT),
        name="hand_over",
    )(*arrays)


def local(fields, out_grad, gain, qkv_weight, out_weight, window_bias):
    tables = window_bias.transpose(0, 2, 1, 3).reshape(2, HEADS, 2, FLAT, 128)
    tables = with_layout_constraint(tables, Layout((0, 1, 3, 2, 4)))
    tables = tables.transpose(0, 1, 3, 2, 4).reshape(2 * 2 * HEADS * FLAT, 128)
    results = block(
        fields.transpose(0, 2, 1, 3), out_grad.transpose(0, 2, 1, 3), gain, qkv_weight, out_weight, tables
    )
    input_grad, qkv_grad, out_weight_grad, gain_grad, bias = hand_over(results)
    bias = bias.reshape(2, HEADS, FLAT, 2, 128).transpose(0, 1, 3, 2, 4)
    return (
        input_grad.transpose(0, 2, 1, 3),
        qkv_grad,
        out_weight_grad,
        gain_grad.reshape(WIDTH),
        bias.reshape(2, HEADS, 2, TOKENS * TOKENS).transpose(0, 2, 1, 3),
    )


def solution(mesh):
    in_specs = (
        P(None, "lat", "lon", None),
        P(None, "lat", "lon", None),
        P(),
        P(),
        P(),
        P("lat", None, None, None),
    )
    out_specs = (P(None, "lat", "lon", None), P(), P(), P(), P("lat", None, None, None))
    return jax.shard_map(local, mesh=mesh, in_specs=in_specs, out_specs=out_specs, check_vma=False)
```

time: 97.1 us -> 75.6 us (0.78)
  local copies, waits for them, and re-layouts: 22.6 us -> 0 us
  Pallas kernels: 73.5 us -> 74.8 us
    reshape x4 -> x0, local copies, waits for them, and re-layouts: 12.4 us -> none  [the longest x2 6.38 us: local(): tables = window_bias.reshape(2, 2, HEADS, TOKENS, TOKENS)]
    unnamed x13 -> x0, local copies, waits for them, and re-layouts: 10.1 us -> none
    pallas_call x1 -> x2, Pallas kernels: 73.5 us -> 74.8 us  [the longest x1 71.7 us: block(): pl.pallas_call(kernel, out_shape=(jax.ShapeDtypeStruct(cells, BF16), jax....]
where the time goes in v3:
time: 75.6 us; the launch traced here: 75.4 us
  Pallas kernels  74.8 us (99%)
    pallas_call x1, Pallas kernels, block(): pl.pallas_call(kernel, out_shape=(jax.ShapeDtypeStruct(cells, BF16), jax....  71.7 us
    pallas_call x1, Pallas kernels, hand_over(): pl.pallas_call(hand_over_kernel, out_shape=tuple((jax.ShapeDtypeStruct(a....  3.03 us

profile of v3, /device:TPU:1, one launch (start us, length us, event | category | flops | bytes accessed | tf_op | source)
XLA Modules:
  0.0 75.4 jit_solution(6803458920052101376)
XLA Ops:
  0.6 71.7 %block.1 = (bf16[4,12,24,192]{3,2,1,0:T(8,128)(2,1)}, f32[192,576]{1,0:T(8,128)}, f32[192,192]{1,0:T(8,128)}, f32[1,192]{1,0:T(1,128)}, f32[3888,128]{1,0:T(8,128)}) custom-call(bf16[4,12,24,192]{3,2,1,0:T(8,128)(2,1)} %bitcast.20, bf16[4,12,24,192]{3,2,1,0:T(8,128)(2,1)} %bitcast.21, f32[1,192]{1,0:T(1,128)} %bitcast.22, bf16[192,576]{1,0:T(8,128)(2,1)} %qkv_ref.1, ...), custom_call_target="tpu_custom_call" | custom-call | tf_op jit(solution)/shard_map/block/pallas_call | solution.py:661
  72.4 3.0 %hand_over.1 = (bf16[4,12,24,192]{3,2,1,0:T(8,128)(2,1)}, f32[192,576]{1,0:T(8,128)}, f32[192,192]{1,0:T(8,128)}, f32[1,192]{1,0:T(1,128)}, f32[3888,128]{1,0:T(8,128)}) custom-call(bf16[4,12,24,192]{3,2,1,0:T(8,128)(2,1)} %get-tuple-element.15.refs_0_, f32[192,576]{1,0:T(8,128)} %get-tuple-element.16.refs_1_, f32[192,192]{1,0:T(8,128)} %get-tuple-element.17.refs_2_, ...), custom_call_target="tpu_custom_call" | custom-call | tf_op jit(solution)/shard_map/hand_over/pallas_call | solution.py:744

commit v4 on v3

--- a/solution.py
+++ b/solution.py
@@ -164,13 +164,13 @@
         at = slice(h * TOKENS, (h + 1) * TOKENS)
         attended_sum = jnp.where(own[h], attended_all[at], attended_sum)
         queries_sum = jnp.where(own[h], queries_grad_all[at], queries_sum)
-    attended_t = jnp.transpose(attended_sum).astype(BF16)
-    queries_grad_t = (jnp.transpose(queries_sum) * scale).astype(BF16)
+    attended_t = jnp.transpose(attended_sum.astype(BF16))
+    queries_grad_t = jnp.transpose((queries_sum * scale).astype(BF16))
     projected_grad_t = jnp.concatenate([queries_grad_t] + keys_parts + values_parts, axis=0)
     weight_acc[3 * WIDTH :, :] += dot(attended_t, upstream)
     weight_acc[: 3 * WIDTH, :] += dot(projected_grad_t, normed)
     shifted_t = dot(qkv_ref[...], projected_grad_t)
-    grad = jnp.transpose(shifted_t).astype(BF16).astype(F32)
+    grad = jnp.transpose(shifted_t.astype(BF16)).astype(F32)
     product = grad * standard
     gain_acc[...] += jnp.sum(product, axis=0, keepdims=True)
     scaled = grad * gain
@@ -226,16 +226,15 @@
             masked_hi[h, at + 36 : at + 72, :] = rows
 
 
-def join_sums(bias_acc):
+def join_sums(bias_acc, own_acc):
     acc_lo, acc_hi = bias_acc
+    own_lo, own_hi = own_acc
     lane = lax.broadcasted_iota(jnp.int32, (36, 128), 1)
     for h in range(HEADS):
         for at in (0, HALF):
             second = slice(at + 36, at + 72)
-            lo, hi = pltpu.roll(acc_lo[h, second, :], 92, 1), pltpu.roll(acc_hi[h, second, :], 92, 1)
-            acc_lo[h, at : at + 36, :] += jnp.where(lane < 92, lo, hi)
-            acc_lo[h, second, :] = jnp.zeros((36, 128), F32)
-            acc_hi[h, second, :] = jnp.zeros((36, 128), F32)
+            lo, hi = pltpu.roll(own_lo[h, second, :], 92, 1), pltpu.roll(own_hi[h, second, :], 92, 1)
+            acc_lo[h, at : at + 36, :] += own_lo[h, at : at + 36, :] + jnp.where(lane < 92, lo, hi)
 
 
 def fold(w, bias_acc, flat, src):
@@ -315,10 +314,10 @@
 
 def kernel(
     fields_hbm, grad_hbm, gain_ref, qkv_ref, out_w_ref, bias_hbm,
-    input_grad_hbm, qkv_grad_ref, out_grad_ref, gain_grad_ref, bias_grad_hbm,
-    fields, grads, bias, bias_out, cells_out, query_t,
+    cells_out, qkv_grad_ref, out_grad_ref, gain_grad_ref, bias_out,
+    fields, grads, bias, query_t,
     a_send, a_recv, b_recv, c_recv, pack32, corner32,
-    win, masked_lo, masked_hi, acc_lo, acc_hi, weight_acc, gain_acc, flat,
+    win, masked_lo, masked_hi, acc_lo, acc_hi, own_lo, own_hi, weight_acc, gain_acc, flat,
     tiles, d_send, e_send, d_recv, e_recv, f_recv,
     src0, src1, src2, src3, src4, core0, core1, core2, core3, core4,
     xb0, xb1, xb2, xb3, xb4, zb0, zb1, zb2, zb3, zb4, out0, out1, out2, out3, out4,
@@ -385,11 +384,6 @@
     for k, own in enumerate((fields, grads)):
         put_cells(own, win, k)
     loads[2].wait()
-    for c in b_copies:
-        c.wait()
-    for k in range(2):
-        put_east(b_recv, win, k)
-
     srcs = (src0, src1, src2, src3, src4)
     core_bufs = (core0, core1, core2, core3, core4)
     x_bufs = (xb0, xb1, xb2, xb3, xb4)
@@ -472,21 +466,15 @@
         gx_copy(c).wait()
         gc_copy(c).start()
 
-    def bias_store(g):
-        part = pl.ds(g * 2 * HEADS * FLAT, 2 * HEADS * FLAT)
-        return pltpu.make_async_copy(bias_out.at[part], bias_grad_hbm.at[part], local_sem.at[3 + g])
-
     def finish(c):
         gc_copy(c).wait()
         g, w = BIAS_CHUNKS[c]
         unfold(g, w, outs[c], flat, bias_out)
-        if w:
-            bias_store(g).start()
 
     @pl.loop(0, 6)
     def _(t):
         early = jnp.where(t < 4, 1, 0)
-        g = early * (2 - t % 2)
+        g = early * (1 + t % 2)
         w = early * (t // 2) + (1 - early) * (t - 4)
 
         @pl.when(t == 4)
@@ -508,23 +496,31 @@
             acc_lo[...] = jnp.zeros_like(acc_lo)
             acc_hi[...] = jnp.zeros_like(acc_hi)
 
-        def run(n):
-            window(
-                win, w, g, n, gain_ref[...], qkv_ref, query_t, out_w_ref, masked, bias_acc, weight_acc, gain_acc
-            )
+        def run(n, acc):
+            window(win, w, g, n, gain_ref[...], qkv_ref, query_t, out_w_ref, masked, acc, weight_acc, gain_acc)
 
         @pl.when((g == 2) & last)
         def _():
             mask_bias(masked, bias, w, g, lat)
             double_mask(masked)
-            run(0)
-            join_sums(bias_acc)
+            own_lo[...] = jnp.zeros_like(own_lo)
+            own_hi[...] = jnp.zeros_like(own_hi)
+            run(0, (own_lo, own_hi))
+            join_sums(bias_acc, (own_lo, own_hi))
 
         @pl.when(g < 2)
         def _():
             mask_bias(masked, bias, w, g, lat)
-            run(0)
-            run(1)
+            run(0, bias_acc)
+
+            @pl.when(t == 0)
+            def _():
+                for c in b_copies:
+                    c.wait()
+                for k in range(2):
+                    put_east(b_recv, win, k)
+
+            run(1, bias_acc)
 
         @pl.when(t == 1)
         def _():
@@ -595,21 +591,6 @@
     gather_z(2)
     gather_x(1)
     gather_core(0)
-    wait(lat_copies)
-    total = lat_buf[0].astype(F32)
-    for i in range(1, LATS):
-        total = total + lat_buf[i].astype(F32)
-    outs[4][mine] = total.astype(BF16)
-    start(gz_copies(4))
-    gather_x(3)
-    gather_x(2)
-    gather_core(1)
-    finish(0)
-    gather_x(4)
-    finish(1)
-    gather_core(3)
-    gather_core(2)
-
     d_copy.wait()
 
     @pl.when(lat > 0)
@@ -621,8 +602,6 @@
     def _():
         e_copy.wait_recv()
         f_copy.wait_recv()
-
-    gather_core(4)
 
     @pl.loop(0, LEVELS)
     def _(lev):
@@ -637,15 +616,25 @@
             tiles[lev, col, 18:24, :] = jnp.where(last, tiles[lev, col, 18:24, :], cells)
             cells_out[lev, col] = tiles[lev, col].astype(BF16)
 
-    cells_store = pltpu.make_async_copy(cells_out, input_grad_hbm, local_sem.at[7])
-    cells_store.start()
+    finish(0)
+    gather_x(3)
+    gather_x(2)
+    gather_core(1)
+    wait(lat_copies)
+    total = lat_buf[0].astype(F32)
+    for i in range(1, LATS):
+        total = total + lat_buf[i].astype(F32)
+    outs[4][mine] = total.astype(BF16)
+    start(gz_copies(4))
+    finish(1)
+    gather_core(3)
+    gather_core(2)
+    gather_x(4)
     finish(2)
     finish(3)
+    gather_core(4)
     gc_copy(4).wait()
     unfold_weights(outs[4], weight_acc, qkv_grad_ref, out_grad_ref, gain_grad_ref)
-    for g in range(2):
-        bias_store(g).wait()
-    cells_store.wait()
 
 
 def block(fields, out_grad, gain, qkv, out_weight, bias):
@@ -661,20 +650,18 @@
     return pl.pallas_call(
         kernel,
         out_shape=(
-            jax.ShapeDtypeStruct(cells, BF16),
-            jax.ShapeDtypeStruct((WIDTH, 3 * WIDTH), F32),
-            jax.ShapeDtypeStruct((WIDTH, WIDTH), F32),
-            jax.ShapeDtypeStruct((1, WIDTH), F32),
-            jax.ShapeDtypeStruct(tables, F32),
+            pltpu.VMEM(cells, BF16),
+            pltpu.VMEM((WIDTH, 3 * WIDTH), F32),
+            pltpu.VMEM((WIDTH, WIDTH), F32),
+            pltpu.VMEM((1, WIDTH), F32),
+            pltpu.VMEM(tables, F32),
         ),
         in_specs=[hbm, hbm, vmem, vmem, vmem, hbm],
-        out_specs=(hbm, vmem, vmem, vmem, hbm),
+        out_specs=(vmem,) * 5,
         scratch_shapes=[
             pltpu.VMEM(cells, BF16),
             pltpu.VMEM(cells, BF16),
             pltpu.VMEM(tables, F32),
-            pltpu.VMEM(tables, F32),
-            pltpu.VMEM(cells, BF16),
             pltpu.VMEM((WIDTH, WIDTH), BF16),
             pltpu.VMEM((LEVELS, 96, 2 * WIDTH), BF16),
             pltpu.VMEM((LEVELS, 64, 2 * WIDTH), BF16),
@@ -683,6 +670,8 @@
             pltpu.VMEM((LEVELS, 96, 2 * WIDTH), F32),
             pltpu.VMEM((LEVELS, 32, 2 * WIDTH), F32),
             pltpu.VMEM((2, 2, 3, 2, 2, 2, HALF, 128), F32),
+            pltpu.VMEM((HEADS, TOKENS, 128), F32),
+            pltpu.VMEM((HEADS, TOKENS, 128), F32),
             pltpu.VMEM((HEADS, TOKENS, 128), F32),
             pltpu.VMEM((HEADS, TOKENS, 128), F32),
             pltpu.VMEM((HEADS, TOKENS, 128), F32),
@@ -715,40 +704,22 @@
 
 
 def hand_over_kernel(*refs):
-    count = (len(refs) - 2) // 3
-    sources, targets, held = refs[:count], refs[count : 2 * count], refs[2 * count : 3 * count]
-    load_sem, store_sem = refs[-2:]
-    loads, stores = [], []
-    for k, (source, there, target) in enumerate(zip(sources, held, targets)):
-        parts = [None]
-        if source.shape[0] == 2 * 2 * HEADS * FLAT:
-            parts = [pl.ds(part * 1296, 1296) for part in range(3)]
-        elif len(source.shape) == 4:
-            parts = [pl.ds(part * 2, 2) for part in range(2)]
-        for p, part in enumerate(parts):
-            a, b, c = (source, there, target) if part is None else (source.at[part], there.at[part], target.at[part])
-            loads.append(pltpu.make_async_copy(a, b, load_sem.at[k, p]))
-            stores.append(pltpu.make_async_copy(b, c, store_sem.at[k, p]))
-    for c in loads:
+    count = (len(refs) - 1) // 2
+    copies = [pltpu.make_async_copy(a, b, refs[-1].at[k]) for k, (a, b) in enumerate(zip(refs, refs[count:-1]))]
+    for c in copies:
         c.start()
-    for a, b in zip(loads, stores):
-        a.wait()
-        b.start()
-    for c in stores:
+    for c in copies:
         c.wait()
 
 
 def hand_over(arrays):
-    hbm = pl.BlockSpec(memory_space=pl.ANY)
-    dma = pltpu.SemaphoreType.DMA
     return pl.pallas_call(
         hand_over_kernel,
         out_shape=tuple(jax.ShapeDtypeStruct(a.shape, a.dtype) for a in arrays),
-        in_specs=[hbm] * len(arrays),
-        out_specs=(hbm,) * len(arrays),
-        scratch_shapes=[pltpu.VMEM(a.shape, a.dtype) for a in arrays]
-        + [dma((len(arrays), 3)), dma((len(arrays), 3))],
-        compiler_params=pltpu.CompilerParams(vmem_limit_bytes=VMEM_LIMIT),
+        in_specs=[pl.BlockSpec(memory_space=pltpu.VMEM)] * len(arrays),
+        out_specs=(pl.BlockSpec(memory_space=pl.ANY),) * len(arrays),
+        scratch_shapes=[pltpu.SemaphoreType.DMA((len(arrays),))],
+        compiler_params=pltpu.CompilerParams(vmem_limit_bytes=8 * 1024 * 1024),
         name="hand_over",
     )(*arrays)
 

time: 75.6 us -> 71.8 us (0.950)
  Pallas kernels: 74.8 us -> 71 us
    pallas_call x1, Pallas kernels: 71.7 us -> 69.2 us  [block(): pl.pallas_call(kernel, out_shape=(pltpu.VMEM(cells, BF16), pltpu.VMEM((WI...]
    pallas_call x1, Pallas kernels: 3.03 us -> 1.75 us  [hand_over(): pl.pallas_call(hand_over_kernel, out_shape=tuple((jax.ShapeDtypeStruct(a....]
where the time goes in v4:
time: 71.8 us; the launch traced here: 71.6 us
  Pallas kernels  71 us (99%)
    pallas_call x1, Pallas kernels, block(): pl.pallas_call(kernel, out_shape=(pltpu.VMEM(cells, BF16), pltpu.VMEM((WI...  69.2 us
    pallas_call x1, Pallas kernels, hand_over(): pl.pallas_call(hand_over_kernel, out_shape=tuple((jax.ShapeDtypeStruct(a....  1.75 us

profile of v4, /device:TPU:1, one launch (start us, length us, event | category | flops | bytes accessed | tf_op | source)
XLA Modules:
  0.0 71.6 jit_solution(3735217089159004854)
XLA Ops:
  0.6 69.2 %block.1 = (bf16[4,12,24,192]{3,2,1,0:T(8,128)(2,1)S(1)}, f32[192,576]{1,0:T(8,128)S(1)}, f32[192,192]{1,0:T(8,128)S(1)}, f32[1,192]{1,0:T(1,128)S(1)}, f32[3888,128]{1,0:T(8,128)S(1)}) custom-call(bf16[4,12,24,192]{3,2,1,0:T(8,128)(2,1)} %bitcast.20, bf16[4,12,24,192]{3,2,1,0:T(8,128)(2,1)} %bitcast.21, f32[1,192]{1,0:T(1,128)} %bitcast.22, ...), custom_call_target="tpu_custom_call" | custom-call | tf_op jit(solution)/shard_map/block/pallas_call | solution.py:650
  69.9 1.8 %hand_over.1 = (bf16[4,12,24,192]{3,2,1,0:T(8,128)(2,1)}, f32[192,576]{1,0:T(8,128)}, f32[192,192]{1,0:T(8,128)}, f32[1,192]{1,0:T(1,128)}, f32[3888,128]{1,0:T(8,128)}) custom-call(bf16[4,12,24,192]{3,2,1,0:T(8,128)(2,1)S(1)} %get-tuple-element.15.refs_0_, f32[192,576]{1,0:T(8,128)S(1)} %get-tuple-element.16.refs_1_, ...), custom_call_target="tpu_custom_call" | custom-call | tf_op jit(solution)/shard_map/hand_over/pallas_call | solution.py:716

commit v5 on v4

--- a/solution.py
+++ b/solution.py
@@ -343,7 +343,7 @@
     loads = [
         pltpu.make_async_copy(fields_hbm, fields, local_sem.at[0]),
         pltpu.make_async_copy(grad_hbm, grads, local_sem.at[1]),
-        pltpu.make_async_copy(bias_hbm, bias, local_sem.at[2]),
+        pltpu.make_async_copy(bias_hbm, bias.at[pl.ds(0, 2 * 2 * HEADS * FLAT)], local_sem.at[2]),
     ]
     for c in loads:
         c.start()
@@ -646,7 +646,7 @@
         return [pltpu.VMEM((count, rows, 128), BF16) for rows in CHUNK_ROWS]
 
     cells = (LEVELS, COLS, ROWS, WIDTH)
-    tables = (2 * 2 * HEADS * FLAT, 128)
+    padded = (2 * 2 * HEADS * FLAT + 144, 128)
     return pl.pallas_call(
         kernel,
         out_shape=(
@@ -654,14 +654,14 @@
             pltpu.VMEM((WIDTH, 3 * WIDTH), F32),
             pltpu.VMEM((WIDTH, WIDTH), F32),
             pltpu.VMEM((1, WIDTH), F32),
-            pltpu.VMEM(tables, F32),
+            pltpu.VMEM(padded, F32),
         ),
         in_specs=[hbm, hbm, vmem, vmem, vmem, hbm],
         out_specs=(vmem,) * 5,
         scratch_shapes=[
             pltpu.VMEM(cells, BF16),
             pltpu.VMEM(cells, BF16),
-            pltpu.VMEM(tables, F32),
+            pltpu.VMEM(padded, F32),
             pltpu.VMEM((WIDTH, WIDTH), BF16),
             pltpu.VMEM((LEVELS, 96, 2 * WIDTH), BF16),
             pltpu.VMEM((LEVELS, 64, 2 * WIDTH), BF16),
@@ -670,15 +670,15 @@
             pltpu.VMEM((LEVELS, 96, 2 * WIDTH), F32),
             pltpu.VMEM((LEVELS, 32, 2 * WIDTH), F32),
             pltpu.VMEM((2, 2, 3, 2, 2, 2, HALF, 128), F32),
-            pltpu.VMEM((HEADS, TOKENS, 128), F32),
-            pltpu.VMEM((HEADS, TOKENS, 128), F32),
-            pltpu.VMEM((HEADS, TOKENS, 128), F32),
-            pltpu.VMEM((HEADS, TOKENS, 128), F32),
-            pltpu.VMEM((HEADS, TOKENS, 128), F32),
-            pltpu.VMEM((HEADS, TOKENS, 128), F32),
+            pltpu.VMEM((HEADS + 1, TOKENS, 128), F32),
+            pltpu.VMEM((HEADS + 1, TOKENS, 128), F32),
+            pltpu.VMEM((HEADS + 1, TOKENS, 128), F32),
+            pltpu.VMEM((HEADS + 1, TOKENS, 128), F32),
+            pltpu.VMEM((HEADS + 1, TOKENS, 128), F32),
+            pltpu.VMEM((HEADS + 1, TOKENS, 128), F32),
             pltpu.VMEM((4 * WIDTH, WIDTH), F32),
             pltpu.VMEM((1, WIDTH), F32),
-            pltpu.VMEM((1024, 128), F32),
+            pltpu.VMEM((1152, 128), F32),
             pltpu.VMEM(cells, F32),
             pltpu.VMEM((LEVELS, 3, ROWS, WIDTH), BF16),
             pltpu.VMEM((LEVELS, 96, WIDTH), BF16),
@@ -705,7 +705,10 @@
 
 def hand_over_kernel(*refs):
     count = (len(refs) - 1) // 2
-    copies = [pltpu.make_async_copy(a, b, refs[-1].at[k]) for k, (a, b) in enumerate(zip(refs, refs[count:-1]))]
+    copies = [
+        pltpu.make_async_copy(a.at[pl.ds(0, b.shape[0])], b, refs[-1].at[k])
+        for k, (a, b) in enumerate(zip(refs, refs[count:-1]))
+    ]
     for c in copies:
         c.start()
     for c in copies:
@@ -715,7 +718,9 @@
 def hand_over(arrays):
     return pl.pallas_call(
         hand_over_kernel,
-        out_shape=tuple(jax.ShapeDtypeStruct(a.shape, a.dtype) for a in arrays),
+        out_shape=tuple(
+            jax.ShapeDtypeStruct((min(a.shape[0], 2 * 2 * HEADS * FLAT), *a.shape[1:]), a.dtype) for a in arrays
+        ),
         in_specs=[pl.BlockSpec(memory_space=pltpu.VMEM)] * len(arrays),
         out_specs=(pl.BlockSpec(memory_space=pl.ANY),) * len(arrays),
         scratch_shapes=[pltpu.SemaphoreType.DMA((len(arrays),))],

time: 71.8 us -> 72 us (level)
  no operation moved by 1% of the time
where the time goes in v5:
time: 72 us; the launch traced here: 71.8 us
  Pallas kernels  71.1 us (99%)
    pallas_call x1, Pallas kernels, block(): pl.pallas_call(kernel, out_shape=(pltpu.VMEM(cells, BF16), pltpu.VMEM((WI...  69.4 us
    pallas_call x1, Pallas kernels, hand_over(): pl.pallas_call(hand_over_kernel, out_shape=tuple((jax.ShapeDtypeStruct((m...  1.75 us

profile of v5, /device:TPU:1, one launch (start us, length us, event | category | flops | bytes accessed | tf_op | source)
XLA Modules:
  0.0 71.8 jit_solution(18114641002705076715)
XLA Ops:
  0.6 69.4 %block.1 = (bf16[4,12,24,192]{3,2,1,0:T(8,128)(2,1)S(1)}, f32[192,576]{1,0:T(8,128)S(1)}, f32[192,192]{1,0:T(8,128)S(1)}, f32[1,192]{1,0:T(1,128)S(1)}, f32[4032,128]{1,0:T(8,128)S(1)}) custom-call(bf16[4,12,24,192]{3,2,1,0:T(8,128)(2,1)} %bitcast.20, bf16[4,12,24,192]{3,2,1,0:T(8,128)(2,1)} %bitcast.21, f32[1,192]{1,0:T(1,128)} %bitcast.22, ...), custom_call_target="tpu_custom_call" | custom-call | tf_op jit(solution)/shard_map/block/pallas_call | solution.py:650
  70.0 1.8 %hand_over.1 = (bf16[4,12,24,192]{3,2,1,0:T(8,128)(2,1)}, f32[192,576]{1,0:T(8,128)}, f32[192,192]{1,0:T(8,128)}, f32[1,192]{1,0:T(1,128)}, f32[3888,128]{1,0:T(8,128)}) custom-call(bf16[4,12,24,192]{3,2,1,0:T(8,128)(2,1)S(1)} %get-tuple-element.15.refs_0_, f32[192,576]{1,0:T(8,128)S(1)} %get-tuple-element.16.refs_1_, ...), custom_call_target="tpu_custom_call" | custom-call | tf_op jit(solution)/shard_map/hand_over/pallas_call | solution.py:719
